TPU v7x, 512 devices: a whole 4x4x16 slice. The times are simulated.
512 devices in a mesh: row: 32 (over y, x, core), col: 16 (over z).
Axes of the slice: x: 4, y: 4, z: 16, core: 2. Of those that a mesh axis runs over, the one named last changes fastest.
Arguments:
- iterate_t: bfloat16 [32, 16, 64, 32768], P(None, 'col', None, 'row'), may hold values from -0.03125 to 0.03125
- vectors: bfloat16 [32768, 256], P(('row', 'col')), may hold values from -6 to 6
- old_factor_t: bfloat16 [512, 32768], P('col', 'row'), may hold values from -5 to 5
Outputs:
- panel: float32 [32768, 256], P(('row', 'col'))
- basis: float32 [768, 32768], P('col', 'row')
All inputs are finite; a program needn't handle non-finite values.
Results may differ from a plain program's by a relative error of at most 0.0013.
Values may be sent and summed in bfloat16 or wider, within the bound.
A program may use at most 64 MiB of HBM per device.

v0:
```python
import jax
import jax.numpy as jnp
from jax import lax
from jax.sharding import PartitionSpec as P

NSTATE = 32768


def body(iterate_t, vectors, old_factor_t):
    flat_iterate = iterate_t.reshape(-1, iterate_t.shape[-1])
    highest = lax.Precision.HIGHEST

    def apply_iterate(vector):
        gathered = lax.all_gather(vector, "row", axis=0, tiled=True)
        return lax.psum_scatter(
            lax.dot_general(
                flat_iterate, gathered, (((0,), (0,)), ((), ())), preferred_element_type=jnp.float32
            ),
            "col",
            scatter_dimension=0,
            tiled=True,
        )

    first_full = apply_iterate(vectors)
    second = apply_iterate(first_full.astype(jnp.bfloat16)).astype(jnp.bfloat16)
    panel = 1.5 * first_full - 0.5 * apply_iterate(second)
    old_gathered = lax.all_gather(old_factor_t, "col", axis=0, tiled=True)
    panel_gathered = lax.all_gather(panel, "col", axis=0, tiled=True)
    old_full = old_gathered.astype(jnp.float32)
    scale_gram = 1.0 / NSTATE
    column = lax.axis_index("col")
    groups = lax.axis_size("col")
    panel_share = panel.shape[1] // groups
    own_panel = lax.dynamic_slice_in_dim(panel_gathered, column * panel_share, panel_share, 1)
    own_old = old_factor_t.astype(jnp.float32)
    old_columns = (
        jnp.concatenate(
            [
                lax.dot_general(
                    old_gathered,
                    old_factor_t,
                    (((1,), (1,)), ((), ())),
                    preferred_element_type=jnp.float32,
                ),
                lax.dot_general(
                    panel_gathered, own_old, (((0,), (1,)), ((), ())), precision=highest
                ),
            ],
            0,
        )
        * scale_gram
    )
    panel_columns = (
        jnp.concatenate(
            [
                jnp.dot(old_full, own_panel, precision=highest),
                lax.dot_general(
                    panel_gathered, own_panel, (((0,), (0,)), ((), ())), precision=highest
                ),
            ],
            0,
        )
        * scale_gram
    )
    summed_old, summed_panel = lax.psum((old_columns, panel_columns), "row")
    left_part, right_part = (
        lax.all_gather(summed_old, "col", axis=1, tiled=True),
        lax.all_gather(summed_panel, "col", axis=1, tiled=True),
    )
    gram = jnp.concatenate([left_part, right_part], 1)
    lower_factor = jnp.linalg.cholesky(gram)
    identity = jnp.eye(gram.shape[0], dtype=jnp.float32)
    inverse = jax.scipy.linalg.solve_triangular(lower_factor, identity, lower=True)
    basis_share = gram.shape[0] // groups
    inverse_rows = lax.dynamic_slice_in_dim(inverse, column * basis_share, basis_share, 0)
    old_count = old_gathered.shape[0]
    basis = jnp.dot(inverse_rows[:, :old_count], old_full, precision=highest)
    basis = basis + lax.dot_general(
        inverse_rows[:, old_count:], panel_gathered, (((1,), (1,)), ((), ())), precision=highest
    )
    return (panel, basis)


def solution(mesh):
    return jax.shard_map(
        body,
        mesh=mesh,
        in_specs=(P(None, "col", None, "row"), P(("row", "col"), None), P("col", "row")),
        out_specs=(P(("row", "col"), None), P("col", "row")),
        check_vma=False,
    )
```

profile of v0, /device:TPU:1, one launch (start us, length us, event | category | flops | bytes accessed | tf_op | source)
XLA Modules:
  0.0 1107.3 jit_solution(5605788853649218226)
XLA Ops:
  7.9 67.0 %all-gather.7.cloned.1.call-done = bf16[2048,256]{1,0:T(8,128)(2,1)} async-done(((bf16[64,256]{1,0:T(8,128)(2,1)}), bf16[2048,256]{1,0:T(8,128)(2,1)}) %all-gather.7.cloned.1.call-update) | async-done | bytes 1048592 | tf_op jit(solution)/shard_map/all_gather | solution.py:14
  75.0 4.7 fusion.64
  79.8 59.3 %reduce-scatter.6.cloned.1.call-done = f32[64,256]{1,0:T(8,128)} async-done(((f32[1024,256]{1,0:T(8,128)}), f32[64,256]{1,0:T(8,128)}) %reduce-scatter.6.cloned.1.call-update) | async-done | bytes 65552 | tf_op jit(solution)/shard_map/reduce_scatter | solution.py:15
  139.1 1.5 convert_element_type.19
  140.6 69.1 %all-gather.9.cloned.1.call-done = bf16[2048,256]{1,0:T(8,128)(2,1)} async-done(((bf16[64,256]{1,0:T(8,128)(2,1)}), bf16[2048,256]{1,0:T(8,128)(2,1)}) %all-gather.9.cloned.1.call-update) | async-done | bytes 1048592 | tf_op jit(solution)/shard_map/all_gather | solution.py:14
  209.8 3.8 convolution_bitcast_fusion.1
  213.5 1.3 copy.14
  214.9 59.3 %reduce-scatter.10.cloned.1.call-done = f32[64,256]{1,0:T(8,128)} async-done(((f32[1024,256]{1,0:T(8,128)}), f32[64,256]{1,0:T(8,128)}) %reduce-scatter.10.cloned.1.call-update) | async-done | bytes 65552 | tf_op jit(solution)/shard_map/reduce_scatter | solution.py:15
  274.3 1.5 convert_element_type.20
  275.8 68.4 %all-gather.11.cloned.1.call-done = bf16[2048,256]{1,0:T(8,128)(2,1)} async-done(((bf16[64,256]{1,0:T(8,128)(2,1)}), bf16[2048,256]{1,0:T(8,128)(2,1)}) %all-gather.11.cloned.1.call-update) | async-done | bytes 1048592 | tf_op jit(solution)/shard_map/all_gather | solution.py:14
  344.2 5.3 convolution_bitcast_fusion
  350.3 58.6 %reduce-scatter.8.cloned.1.call-done = f32[64,256]{1,0:T(8,128)} async-done(((f32[1024,256]{1,0:T(8,128)}), f32[64,256]{1,0:T(8,128)}) %reduce-scatter.8.cloned.1.call-update) | async-done | bytes 65552 | tf_op jit(solution)/shard_map/reduce_scatter | solution.py:15
  408.9 1.5 multiply_subtract_fusion
  410.5 70.2 %all-gather.13.cloned.1.call-done = bf16[512,1024]{1,0:T(8,128)(2,1)} async-done(((bf16[32,1024]{1,0:T(8,128)(2,1)}), bf16[512,1024]{1,0:T(8,128)(2,1)}) %all-gather.13.cloned.1.call-update) | async-done | bytes 1048592 | tf_op jit(solution)/shard_map/all_gather | solution.py:27
  480.7 1.6 fusion.65
  482.3 69.3 %all-gather.15.cloned.1.call-done = f32[1024,256]{1,0:T(8,128)} async-done(((f32[64,256]{1,0:T(8,128)}), f32[1024,256]{1,0:T(8,128)}) %all-gather.15.cloned.1.call-update) | async-done | bytes 1048592 | tf_op jit(solution)/shard_map/all_gather | solution.py:28
  551.6 1.8 fusion.66
  554.1 136.4 %all-reduce.3.cloned.1.call-done = f32[768,32]{0,1:T(8,128)} async-done(((f32[768,32]{0,1:T(8,128)}), f32[768,32]{0,1:T(8,128)}) %all-reduce.3.cloned.1.call-update) | async-done | bytes 98320 | tf_op jit(solution)/shard_map/psum | solution.py:65
  691.6 1.6 fusion.20
  693.1 1.1 fusion.24
  694.3 1.2 convolution_bitcast_fusion.2
  695.5 120.7 %psum.15 = f32[768,16]{0,1:T(8,128)S(1)} all-reduce(f32[768,16]{0,1:T(8,128)S(1)} %maximum_multiply_fusion.1), channel_id=1, replica_groups=mesh['row'=32,'col'=16] {'row'}, use_global_device_ids=true, to_apply=%region_4.0 | all-reduce | flops 12288 | bytes 98304 | tf_op jit(solution)/shard_map/psum | solution.py:65
  816.2 30.3 %all_gather.27 = f32[768,256]{0,1:T(8,128)} all-gather(f32[768,16]{0,1:T(8,128)S(1)} %psum.15), channel_id=1, replica_groups=mesh['row'=32,'col'=16] {'col'}, dimensions={1}, use_global_device_ids=true | all-gather | bytes 835584 | tf_op jit(solution)/shard_map/all_gather | solution.py:68
  846.5 1.6 constant_dynamic-update-slice_fusion.1
  848.2 2.4 copy.12
  850.6 2.0 fusion
  852.6 1.4 copy-done.4
  854.0 11.7 %cholesky.165 = f32[128,128]{1,0:T(8,128)S(1)} custom-call(f32[128,128]{1,0:T(8,128)S(1)} %cholesky.424), custom_call_target="Cholesky" | custom-call | tf_op jit(solution)/shard_map/jit(cholesky)/cholesky | solution.py:71
  865.8 9.8 custom-call.47
  875.8 1.4 constant_dynamic-update-slice_fusion.16
  877.2 1.4 convolution_subtract_fusion.4
  879.3 11.7 %cholesky.188 = f32[128,128]{1,0:T(8,128)S(1)} custom-call(f32[128,128]{1,0:T(8,128)S(1)} %cholesky.428), custom_call_target="Cholesky" | custom-call | tf_op jit(solution)/shard_map/jit(cholesky)/cholesky | solution.py:71
  891.0 10.0 custom-call.48
  901.0 1.3 convolution_dynamic-update-slice_fusion.1
  902.3 1.5 convolution_subtract_fusion.5
  904.6 11.7 %cholesky.354 = f32[128,128]{1,0:T(8,128)S(1)} custom-call(f32[128,128]{1,0:T(8,128)S(1)} %cholesky.433), custom_call_target="Cholesky" | custom-call | tf_op jit(solution)/shard_map/jit(cholesky)/cholesky | solution.py:71
  916.9 9.8 custom-call.49
  926.8 1.2 convolution_dynamic-update-slice_fusion.2
  928.0 1.6 convolution_subtract_fusion.6
  930.3 12.1 %cholesky.373 = f32[128,128]{1,0:T(8,128)S(1)} custom-call(f32[128,128]{1,0:T(8,128)S(1)} %cholesky.438), custom_call_target="Cholesky" | custom-call | tf_op jit(solution)/shard_map/jit(cholesky)/cholesky | solution.py:71
  943.0 9.8 custom-call.50
  952.8 1.2 convolution_dynamic-update-slice_fusion.3
  954.0 1.5 convolution_subtract_fusion.7
  956.1 13.2 %cholesky.392 = f32[128,128]{1,0:T(8,128)} custom-call(f32[128,128]{1,0:T(8,128)} %cholesky.443), custom_call_target="Cholesky" | custom-call | tf_op jit(solution)/shard_map/jit(cholesky)/cholesky | solution.py:71
  969.3 1.5 select_reduce_fusion.1
  971.5 11.3 %custom-call.51 = f32[1,128,128]{1,2,0:T(8,128)} custom-call(f32[1,128,128]{2,1,0:T(8,128)} %get-tuple-element.33), custom_call_target="InvertDiagBlocksLowerTriangular" | custom-call | tf_op jit(solution)/shard_map/jit(cholesky)/cholesky | solution.py:71
  983.8 1.3 convolution_subtract_fusion.8
  985.2 11.9 %cholesky.410 = f32[128,128]{1,0:T(8,128)S(1)} custom-call(f32[128,128]{1,0:T(8,128)S(1)} %convolution_subtract_fusion.8), custom_call_target="Cholesky" | custom-call | tf_op jit(solution)/shard_map/jit(cholesky)/cholesky | solution.py:71
  1002.2 1.6 select_select_fusion
  1003.8 20.6 %while.1 = (s32[]{:T(128)}, f32[768,768]{1,0:T(8,128)}, s32[6,2]{0,1:T(2,128)S(1)}, f32[6,128,128]{2,1,0:T(8,128)}, s32[]{:T(128)}) while((s32[]{:T(128)}, f32[768,768]{1,0:T(8,128)}, s32[6,2]{0,1:T(2,128)S(1)}, f32[6,128,128]{2,1,0:T(8,128)}, s32[]{:T(128)}) %tuple.44), condition=%wide.while_cond, body=%wide.while_body.sunk | while | flops 2 | bytes 132705 | solution.py:73
  1004.4 2.9 bitcast_dynamic-update-slice_fusion.2
  1008.0 2.8 bitcast_dynamic-update-slice_fusion.2
  1011.4 2.8 bitcast_dynamic-update-slice_fusion.2
  1014.8 2.8 bitcast_dynamic-update-slice_fusion.2
  1018.2 2.8 bitcast_dynamic-update-slice_fusion.2
  1021.7 2.8 bitcast_dynamic-update-slice_fusion.2
  1024.4 60.4 %custom-call.52 = f32[6,128,128]{1,2,0:T(8,128)} custom-call(f32[6,128,128]{2,1,0:T(8,128)} %get-tuple-element.9), custom_call_target="InvertDiagBlocksLowerTriangular" | custom-call | tf_op jit(solution)/shard_map/jit(_solve_triangular)/triangular_solve | solution.py:73
  1084.8 1.3 constant_dynamic-update-slice_fusion.6
  1086.1 1.5 convolution_subtract_fusion.2
  1088.2 1.5 convolution_subtract_fusion.3
  1090.2 1.8 convolution_subtract_fusion.1
  1092.5 2.0 fusion.9
  1095.0 2.3 convolution_subtract_fusion
  1098.5 1.8 convolution_add_fusion
  (86 shorter events, 18.0 us)
Async XLA Ops:
  7.2 67.8 %all-gather.7.cloned.1.call-start = ((), (), s32[]{:S(2)}) async-start(), calls=%async_computation.3 | async-start | bytes 1081344 | tf_op jit(solution)/shard_map/all_gather | solution.py:14
  7.9 131.2 %reduce-scatter.6.cloned.1.call-start = ((), (), s32[]{:S(2)}) async-start(), calls=%async_computation.4 | async-start | bytes 1114112 | tf_op jit(solution)/shard_map/reduce_scatter | solution.py:15
  79.8 130.0 %all-gather.9.cloned.1.call-start = ((), (), s32[]{:S(2)}) async-start(), calls=%async_computation.5 | async-start | bytes 1081344 | tf_op jit(solution)/shard_map/all_gather | solution.py:14
  140.6 133.7 %reduce-scatter.10.cloned.1.call-start = ((), (), s32[]{:S(2)}) async-start(), calls=%async_computation.12 | async-start | bytes 1114112 | tf_op jit(solution)/shard_map/reduce_scatter | solution.py:15
  214.9 129.4 %all-gather.11.cloned.1.call-start = ((), (), s32[]{:S(2)}) async-start(), calls=%async_computation.6 | async-start | bytes 1081344 | tf_op jit(solution)/shard_map/all_gather | solution.py:14
  275.7 133.2 %copy-start.11 = (f32[64,256]{1,0:T(8,128)S(1)}, f32[64,256]{1,0:T(8,128)}, u32[]{:S(2)}) copy-start(f32[64,256]{1,0:T(8,128)} %reduce-scatter.6.cloned.1.call-done) | copy-start | bytes 196612
  275.8 204.9 %copy-start.9 = (bf16[32,1024]{1,0:T(8,128)(2,1)S(1)}, bf16[32,1024]{1,0:T(8,128)(2,1)}, u32[]{:S(2)}) copy-start(bf16[32,1024]{1,0:T(8,128)(2,1)} %param.5) | copy-start | bytes 196612
  275.8 133.1 %reduce-scatter.8.cloned.1.call-start = ((), (), s32[]{:S(2)}) async-start(), calls=%async_computation.7 | async-start | bytes 1114112 | tf_op jit(solution)/shard_map/reduce_scatter | solution.py:15
  349.5 131.2 %all-gather.13.cloned.1.call-start = ((), (), s32[]{:S(2)}) async-start(), calls=%async_computation.8 | async-start | bytes 1114112 | tf_op jit(solution)/shard_map/all_gather | solution.py:27
  350.3 201.3 %all-gather.15.cloned.1.call-start = ((), (), s32[]{:S(2)}) async-start(), calls=%async_computation.9 | async-start | bytes 1114112 | tf_op jit(solution)/shard_map/all_gather | solution.py:28
  410.4 280.1 %all-reduce.3.cloned.1.call-start = ((), (), s32[]{:S(2)}) async-start(), calls=%async_computation.10 | async-start | bytes 196608 | tf_op jit(solution)/shard_map/psum | solution.py:65
  551.6 141.5 %copy-start = (f32[1024,256]{1,0:T(8,128)S(1)}, f32[1024,256]{1,0:T(8,128)}, u32[]{:S(2)}) copy-start(f32[1024,256]{1,0:T(8,128)} %all-gather.15.cloned.1.call-done) | copy-start | bytes 3145732
  553.4 140.9 %copy-start.1 = (bf16[512,1024]{1,0:T(8,128)(2,1)S(1)}, bf16[512,1024]{1,0:T(8,128)(2,1)}, u32[]{:S(2)}) copy-start(bf16[512,1024]{1,0:T(8,128)(2,1)} %all-gather.13.cloned.1.call-done) | copy-start | bytes 3145732
  554.1 292.4 %all-gather.17.cloned.1.call-start = ((), (), s32[]{:S(2)}) async-start(), calls=%async_computation.11 | async-start | bytes 1671168 | tf_op jit(solution)/shard_map/all_gather | solution.py:67
  846.5 1.6 copy-start.5
  852.6 1.5 copy-start.4
  878.6 0.7 copy-start.6
  903.9 0.7 copy-start.7
  929.6 0.7 copy-start.8
  1003.8 84.4 %copy-start.3 = (f32[768,768]{1,0:T(8,128)S(1)}, f32[768,768]{1,0:T(8,128)}, u32[]{:S(2)}) copy-start(f32[768,768]{1,0:T(8,128)} %fusion.20) | copy-start | bytes 7077892
  1084.8 2.8 copy-start.10
  1094.5 3.4 copy-start.2
Sparse Core Ops, SparseCore 0:
  11.1 63.8 all-gather.6
  79.9 59.1 reduce-scatter.5
  143.3 66.4 all-gather.8
  215.0 59.2 reduce-scatter.9
  277.8 66.3 all-gather.10
  349.7 59.2 reduce-scatter.7
  411.2 69.4 all-gather.12
  483.6 67.9 all-gather.14
  555.8 134.7 all-reduce.2
  692.4 62.8 all-gather.16
where the time goes:
time: 1120 us; the launch traced here: 1110 us
  waiting for transfers between devices  659 us (59%)
  other arithmetic  200 us (18%)
  blocking collectives  151 us (13%)
  matrix products  48.3 us (4%)
  local copies, waits for them, and re-layouts  30.4 us (3%)
  between operations  18.5 us (2%)
    all_gather x3, waiting for transfers between devices, apply_iterate(): gathered = lax.all_gather(vector, 'row', axis=0, tiled=True)  205 us
    reduce_scatter x3, waiting for transfers between devices, apply_iterate(): lax.psum_scatter(lax.dot_general(flat_iterate, gathered, (((0,), (0,)), (...  177 us
    psum x1, waiting for transfers between devices, body(): summed_old, summed_panel = lax.psum((old_columns, panel_columns), 'row')  136 us
    another operation x22, other arithmetic, body(): lower_factor = jnp.linalg.cholesky(gram)  128 us
    psum x1, blocking collectives, body(): summed_old, summed_panel = lax.psum((old_columns, panel_columns), 'row')  121 us
    all_gather x1, waiting for transfers between devices, body(): old_gathered = lax.all_gather(old_factor_t, 'col', axis=0, tiled=True)  70.2 us
    all_gather x1, waiting for transfers between devices, body(): panel_gathered = lax.all_gather(panel, 'col', axis=0, tiled=True)  69.3 us
    another operation x3, other arithmetic, body(): jax.scipy.linalg.solve_triangular(lower_factor, identity, lower=True)  62 us
  transfers between devices with their start and end apart: 10, of which 9 were waited for; matrix products, arithmetic and copies ran while one was open for 1% of the time, Pallas kernels for 0%

commit v1 on v0

v1 whole, which is shorter than its diff:
```python
import functools

import jax
import jax.numpy as jnp
from jax import lax
from jax.experimental import pallas as pl
from jax.experimental.pallas import tpu as pltpu
from jax.sharding import PartitionSpec as P

NSTATE = 32768
MESH = pl.DeviceIdType.MESH
HIGHEST = lax.Precision.HIGHEST
BF = jnp.bfloat16
F32 = jnp.float32
NT = (((1,), (1,)), ((), ()))


def split3(a):
    hi = a.astype(BF)
    rest = a - hi.astype(F32)
    mid = rest.astype(BF)
    low = (rest - mid.astype(F32)).astype(BF)
    return hi, mid, low


def comm_kernel(
    x, v, old, panel_o, oldall, pall, aout, bcout,
    xt, vsend, vg, part, bufr, bufl, first,
    apart, asib, ash, apl, bcpart, bcsib, bcs, bcr, bcz, zsh, fsh,
    ag_s, ag_r, fw_s, fw_r, rs_s, rs_r, og_s, og_r, pg_s, pg_r, az_s, az_r,
    a_s, a_r, b_s, b_r,
):
    row = lax.axis_index("row")
    z = lax.axis_index("col")
    chip = row // 2
    core = row % 2
    sib = (chip * 2 + 1 - core, z)
    right = (row, (z + 1) % 16)
    left = (row, (z + 15) % 16)

    def plane(d):
        y = (chip // 4 + d // 4) % 4
        w = (chip % 4 + d % 4) % 4
        return y * 4 + w

    def remote(src, dst, ssem, rsem, target):
        return pltpu.make_async_remote_copy(
            src_ref=src, dst_ref=dst, send_sem=ssem, recv_sem=rsem, device_id=target, device_id_type=MESH
        )

    barrier = pltpu.get_barrier_semaphore()

    @pl.loop(1, 16)
    def _(d):
        pl.semaphore_signal(barrier, inc=1, device_id=(plane(d) * 2 + core, z), device_id_type=MESH)
        pl.semaphore_signal(barrier, inc=1, device_id=(row, (z + d) % 16), device_id_type=MESH)

    pl.semaphore_signal(barrier, inc=1, device_id=sib, device_id_type=MESH)

    @pl.loop(0, 16)
    def _(t):
        a = (t % 8) * 4 + t // 8
        pair = jnp.concatenate([x[a, 0], x[a + 2, 0]], 0)
        xt[:, pl.ds(pl.multiple_of(t * 128, 128), 128)] = pair.T

    pl.semaphore_wait(barrier, 31)

    def plane_push(src, dst, ssem, rsem):
        @pl.loop(1, 16)
        def _(d):
            remote(src, dst, ssem, rsem, (plane(d) * 2 + core, z)).start()

    def bulk(ref, ssem, rsem):
        return remote(ref.at[pl.ds(0, 15)], ref.at[pl.ds(0, 15)], ssem, rsem, sib)

    def gather_start(m):
        plane_push(vsend.at[m], vg.at[m, core * 16 + chip], ag_s.at[m], ag_r.at[m])
        vg[m, core * 16 + chip] = vsend[m]

    def product(m, half, add):
        rhs = vg[m, pl.ds(half * 16, 16)].reshape(1024, 256)
        for rb in range(2):
            lhs = xt[pl.ds(rb * 512, 512), pl.ds(pl.multiple_of(half * 1024, 1024), 1024)]
            res = jnp.dot(lhs, rhs, preferred_element_type=F32).reshape(8, 64, 256)
            if add:
                part[m, pl.ds(rb * 8, 8)] += res
            else:
                part[m, pl.ds(rb * 8, 8)] = res

    def gather_product(m):
        wait = bulk(vg.at[m], ag_s.at[m], ag_r.at[m])
        wait.wait_recv()
        span = vg.at[m, pl.ds(core * 16, 16)]
        forward = remote(span, span, fw_s.at[m], fw_r.at[m], sib)
        forward.start()
        product(m, core, False)
        forward.wait_recv()
        product(m, 1 - core, True)
        wait.wait_send()
        forward.wait_send()

    def rs_copy(m, way, s):
        buf, to = (bufr, right) if way == 0 else (bufl, left)
        dest = (z + 8 - s) % 16 if way == 0 else (z + 9 + s) % 16
        return remote(part.at[m, dest], buf.at[m, s], rs_s.at[m, way, s], rs_r.at[m, way, s], to), dest

    def reduce_scatter(m, hook):
        for way in (0, 1):
            rs_copy(m, way, 0)[0].start()
        for s in range(1, 8):
            for way in (0, 1):
                if way == 1 and s == 7:
                    continue
                rs_copy(m, way, s - 1)[0].wait_recv()
                copy, dest = rs_copy(m, way, s)
                buf = bufr if way == 0 else bufl
                part[m, dest] += buf[m, s - 1]
                copy.start()
            hook(s)
        rs_copy(m, 1, 6)[0].wait_recv()
        rs_copy(m, 0, 7)[0].wait_recv()
        res = part[m, z] + bufr[m, 7] + bufl[m, 6]
        for s in range(8):
            rs_copy(m, 0, s)[0].wait_send()
            if s < 7:
                rs_copy(m, 1, s)[0].wait_send()
        return res

    def ring(own, blocks, ssem, rsem):
        def copy(way, s):
            idx = (z - s + 16) % 16 if way == 0 else (z + s) % 16
            return remote(
                own if s == 0 else blocks.at[idx], blocks.at[idx], ssem.at[way, s], rsem.at[way, s],
                right if way == 0 else left,
            )

        def step(s):
            for way in (0, 1):
                if s > 0 and not (way == 1 and s == 8):
                    copy(way, s - 1).wait_recv()
                if s < 8 and not (way == 1 and s == 7):
                    copy(way, s).start()

        def finish():
            for s in range(8):
                copy(0, s).wait_send()
                if s < 7:
                    copy(1, s).wait_send()

        return step, finish

    vsend[0] = v[...]
    gather_start(0)
    old_step, old_finish = ring(old, oldall, og_s, og_r)
    old_step(0)
    oldall[z] = old[...]
    gather_product(0)

    def hook0(s):
        old_step(s)

    first_full = reduce_scatter(0, hook0)
    first[...] = first_full
    vsend[1] = first_full.astype(BF)
    gather_start(1)
    old_step(8)
    old_finish()

    every = oldall[...].reshape(512, 1024)
    share = lax.dot_general(old[...], every, NT, preferred_element_type=F32)
    apart[...] = share.reshape(2, 16, 512)
    a_sib = remote(apart.at[1 - core], asib, a_s.at[0], a_r.at[0], sib)
    a_sib.start()
    gather_product(1)
    a_sib.wait_recv()
    ash[...] = apart[core] + asib[...]
    plane_push(ash, apl.at[chip], a_s.at[1], a_r.at[1])
    apl[chip] = ash[...]
    a_wait = bulk(apl, a_s.at[1], a_r.at[1])
    a_step, a_finish = ring(aout.at[core, z], aout.at[core], az_s, az_r)

    def hook1(s):
        if s == 3:
            a_wait.wait_recv()
            total = apl[0]
            for q in range(1, 16):
                total = total + apl[q]
            aout[core, z] = total * (1.0 / NSTATE)
        if s >= 3:
            a_step(s - 3)

    second = reduce_scatter(1, hook1)
    vsend[2] = second.astype(BF)
    gather_start(2)
    a_step(5)
    gather_product(2)

    a_half = aout.at[core]
    a_forward = remote(a_half, a_half, a_s.at[2], a_r.at[2], sib)

    def hook2(s):
        if s <= 3:
            a_step(5 + s)
        if s == 4:
            a_forward.start()

    third = reduce_scatter(2, hook2)
    panel = 1.5 * first[...] - 0.5 * third
    panel_o[...] = panel
    p_step, p_finish = ring(panel_o, pall, pg_s, pg_r)
    p_step(0)
    pall[z] = panel

    side = z % 2
    doubled = jnp.concatenate([panel, panel], 0)
    rows = lax.broadcasted_iota(jnp.int32, (128, 256), 0)
    doubled = jnp.where(rows // 64 == side, doubled, 0.0).T
    window = oldall[:, :, pl.ds(pl.multiple_of((z // 2) * 128, 128), 128)].reshape(512, 128)
    cross = sum(lax.dot_general(t, window, NT, preferred_element_type=F32) for t in split3(doubled))
    square = lax.dot_general(doubled, doubled, NT, precision=HIGHEST, preferred_element_type=F32)
    bcpart[:, :, :, pl.ds(0, 512)] = cross.reshape(2, 16, 8, 512)
    bcpart[:, :, :, pl.ds(512, 256)] = square.reshape(2, 16, 8, 256)
    b_sib = remote(bcpart.at[1 - core], bcsib, b_s.at[0], b_r.at[0], sib)
    b_sib.start()
    p_step(1)
    b_sib.wait_recv()
    bcs[...] = bcpart[core] + bcsib[...]

    @pl.loop(1, 16)
    def _(d):
        q = plane(d)
        remote(bcs.at[q], bcr.at[chip], b_s.at[1], b_r.at[1], (q * 2 + core, z)).start()

    bcr[chip] = bcs[chip]
    p_step(2)
    p_step(3)
    b_rs = bulk(bcr, b_s.at[1], b_r.at[1])
    b_rs.wait_recv()
    total = bcr[0]
    for q in range(1, 16):
        total = total + bcr[q]
    zsh[...] = total

    @pl.loop(1, 16)
    def _(d):
        remote(zsh, bcz.at[z], b_s.at[2], b_r.at[2], (row, (z + d) % 16)).start()

    bcz[z] = zsh[...]
    p_step(4)
    p_step(5)
    p_step(6)
    b_z = bulk(bcz, b_s.at[2], b_r.at[2])
    b_z.wait_recv()
    total = bcz[0]
    for q in range(1, 16):
        total = total + bcz[q]
    fsh[...] = total * (1.0 / NSTATE)
    plane_push(fsh, bcout.at[core, chip], b_s.at[3], b_r.at[3])
    bcout[core, chip] = fsh[...]
    p_step(7)
    b_ag = bulk(bcout.at[core], b_s.at[3], b_r.at[3])
    b_ag.wait_recv()
    b_half = bcout.at[core]
    b_forward = remote(b_half, b_half, b_s.at[4], b_r.at[4], sib)
    b_forward.start()
    p_step(8)
    p_finish()
    a_finish()
    a_sib.wait_send()
    a_wait.wait_send()
    a_forward.wait_recv()
    a_forward.wait_send()
    b_sib.wait_send()
    b_rs.wait_send()
    b_z.wait_send()
    b_ag.wait_send()
    b_forward.wait_recv()
    b_forward.wait_send()


def inverse_factor(block):
    n = 128
    rows = lax.broadcasted_iota(jnp.int32, (n, n), 0)
    lanes = lax.broadcasted_iota(jnp.int32, (n, n), 1)

    def eight(g, m):
        live = rows < n - 8 * g
        for s in range(8):
            column = m[:, s : s + 1]
            pivot_row = m[s : s + 1, :]
            pivot = m[s : s + 1, s : s + 1]
            factor = jnp.where(live & (rows > s), jnp.broadcast_to(column / pivot, (n, n)), 0.0)
            here = lanes == s
            line = jnp.where(here[s : s + 1, :], 1.0, pivot_row)
            m = jnp.where(here & live & (rows > s), 0.0, m) - factor * line
        m = jnp.concatenate([m[8:], m[:8]], 0)
        return pltpu.roll(m, n - 8, 1)

    m = lax.fori_loop(0, n // 8, eight, block)
    pivots = jnp.sum(jnp.where(rows == lanes, m, 0.0), axis=1, keepdims=True)
    unit = jnp.where(lanes < rows, m, jnp.where(lanes == rows, 1.0, 0.0))
    return unit * lax.rsqrt(pivots)


def basis_kernel(aout, bcout, oldall, pall, basis_o, gram, inv):
    z = lax.axis_index("col")

    @pl.loop(0, 16)
    def _(c):
        for h in range(2):
            gram[pl.ds(pl.multiple_of(c * 32 + h * 16, 16), 16), pl.ds(0, 512)] = aout[h, c]

    gram[pl.ds(512, 256), :] = bcout[...].reshape(256, 768)
    inv[...] = jnp.zeros((768, 768), F32)

    def dot(a, b):
        return jnp.dot(a, b, precision=HIGHEST, preferred_element_type=F32)

    def dot_nt(a, b):
        return lax.dot_general(a, b, NT, precision=HIGHEST, preferred_element_type=F32)

    for j in range(6):
        lo, hi = j * 128, (j + 1) * 128
        w = inverse_factor(gram[lo:hi, lo:hi])
        inv[lo:hi, lo:hi] = w
        if j > 0:
            inv[lo:hi, 0:lo] = dot(w, inv[lo:hi, 0:lo])
        if j < 5:
            factor = dot_nt(gram[hi:, lo:hi], w)
            for k in range(j + 1, 6):
                top = (k - j - 1) * 128
                gram[k * 128 :, k * 128 : (k + 1) * 128] -= dot_nt(factor[top:], factor[top : top + 128])
            inv[hi:, 0:hi] -= dot(factor, inv[lo:hi, 0:hi])

    mine = inv[pl.ds(pl.multiple_of(z * 48, 16), 48), :]
    every = oldall[...].reshape(512, 1024)
    res = dot_nt(mine[:, 512:], pall[...].reshape(1024, 256))
    for t in split3(mine[:, :512]):
        res = res + jnp.dot(t, every, preferred_element_type=F32)
    basis_o[...] = res


def body(iterate_t, vectors, old_factor_t):
    vm = pl.BlockSpec(memory_space=pltpu.VMEM)
    dma = pltpu.SemaphoreType.DMA
    out = jax.ShapeDtypeStruct
    panel, oldall, pall, aout, bcout = pl.pallas_call(
        comm_kernel,
        out_shape=(
            out((64, 256), F32),
            out((16, 32, 1024), BF),
            out((16, 64, 256), F32),
            out((2, 16, 16, 512), F32),
            out((2, 16, 8, 768), F32),
        ),
        in_specs=[vm] * 3,
        out_specs=(vm,) * 5,
        scratch_shapes=[
            pltpu.VMEM((1024, 2048), BF),
            pltpu.VMEM((3, 64, 256), BF),
            pltpu.VMEM((3, 32, 64, 256), BF),
            pltpu.VMEM((3, 16, 64, 256), F32),
            pltpu.VMEM((3, 8, 64, 256), F32),
            pltpu.VMEM((3, 7, 64, 256), F32),
            pltpu.VMEM((64, 256), F32),
            pltpu.VMEM((2, 16, 512), F32),
            pltpu.VMEM((16, 512), F32),
            pltpu.VMEM((16, 512), F32),
            pltpu.VMEM((16, 16, 512), F32),
            pltpu.VMEM((2, 16, 8, 768), F32),
            pltpu.VMEM((16, 8, 768), F32),
            pltpu.VMEM((16, 8, 768), F32),
            pltpu.VMEM((16, 8, 768), F32),
            pltpu.VMEM((16, 8, 768), F32),
            pltpu.VMEM((8, 768), F32),
            pltpu.VMEM((8, 768), F32),
            dma((3,)), dma((3,)), dma((3,)), dma((3,)),
            dma((3, 2, 8)), dma((3, 2, 8)),
            dma((2, 8)), dma((2, 8)),
            dma((2, 8)), dma((2, 8)),
            dma((2, 8)), dma((2, 8)),
            dma((3,)), dma((3,)),
            dma((5,)), dma((5,)),
        ],
        compiler_params=pltpu.CompilerParams(
            collective_id=0, has_side_effects=True, vmem_limit_bytes=48 << 20
        ),
        name="sign_step",
    )(iterate_t, vectors, old_factor_t)
    basis = pl.pallas_call(
        basis_kernel,
        out_shape=out((48, 1024), F32),
        in_specs=[vm] * 4,
        out_specs=vm,
        scratch_shapes=[pltpu.VMEM((768, 768), F32), pltpu.VMEM((768, 768), F32)],
        compiler_params=pltpu.CompilerParams(vmem_limit_bytes=48 << 20),
        name="recompress",
    )(aout, bcout, oldall, pall)
    return panel, basis


def solution(mesh):
    return jax.shard_map(
        body,
        mesh=mesh,
        in_specs=(P(None, "col", None, "row"), P(("row", "col"), None), P("col", "row")),
        out_specs=(P(("row", "col"), None), P("col", "row")),
        check_vma=False,
    )
```

time: 1120 us -> 267 us (0.24); the launches traced: 1110 us -> 266 us
  waiting for transfers between devices: 659 us -> 0 us
  Pallas kernels: 0 us -> 263 us
  other arithmetic: 200 us -> 0 us
  blocking collectives: 151 us -> 0 us
  matrix products: 48.3 us -> 0 us
  local copies, waits for them, and re-layouts: 30.4 us -> 2.22 us
  between operations: 18.5 us -> 0.65 us
    all_gather x6 -> x0, waiting for transfers between devices: 344 us -> none  [the longest x3 205 us: apply_iterate(): gathered = lax.all_gather(vector, 'row', axis=0, tiled=True)]
    pallas_call x0 -> x2, Pallas kernels: none -> 263 us  [the longest x1 182 us: body(): pl.pallas_call(comm_kernel, out_shape=(out((64, 256), F32), out((16, 32,...]
    another operation x25 -> x0, other arithmetic: 190 us -> none  [the longest x22 128 us: body(): lower_factor = jnp.linalg.cholesky(gram)]
    reduce_scatter x3 -> x0, waiting for transfers between devices: 177 us -> none  [apply_iterate(): lax.psum_scatter(lax.dot_general(flat_iterate, gathered, (((0,), (0,)), (...]
    psum x1 -> x0, waiting for transfers between devices: 136 us -> none  [body(): summed_old, summed_panel = lax.psum((old_columns, panel_columns), 'row')]
    psum x1 -> x0, blocking collectives: 121 us -> none  [body(): summed_old, summed_panel = lax.psum((old_columns, panel_columns), 'row')]
    all_gather x1 -> x0, blocking collectives: 30.3 us -> none  [body(): lax.all_gather(summed_panel, 'col', axis=1, tiled=True)]
    another operation x21 -> x0, matrix products: 26.4 us -> none  [the longest x10 13.4 us: body(): lower_factor = jnp.linalg.cholesky(gram)]
  transfers between devices with their start and end apart: 10 -> 0, of which waited for: 9 -> 0; matrix products, arithmetic and copies ran while one was open for 1% -> 0% of each run, Pallas kernels for 0% -> 0%
where the time goes in v1:
time: 267 us; the launch traced here: 266 us
  Pallas kernels  263 us (99%)
    pallas_call x1, Pallas kernels, body(): pl.pallas_call(comm_kernel, out_shape=(out((64, 256), F32), out((16, 32,...  182 us
    pallas_call x1, Pallas kernels, body(): pl.pallas_call(basis_kernel, out_shape=out((48, 1024), F32), in_specs=[vm...  81.9 us

profile of v1, /device:TPU:1, one launch (start us, length us, event | category | flops | bytes accessed | tf_op | source)
XLA Modules:
  0.0 266.3 jit_solution(12372727466613450062)
XLA Ops:
  0.6 0.0 copy-start
  0.6 0.8 copy-done
  1.5 0.0 copy-start.1
  1.5 0.8 copy-done.1
  2.2 181.5 %sign_step.1 = (f32[64,256]{1,0:T(8,128)S(1)}, bf16[16,32,1024]{2,1,0:T(8,128)(2,1)S(1)}, f32[16,64,256]{2,1,0:T(8,128)S(1)}, f32[2,16,16,512]{3,2,1,0:T(8,128)S(1)}, f32[2,16,8,768]{3,2,1,0:T(8,128)S(1)}) custom-call(bf16[32,1,64,1024]{3,2,1,0:T(8,128)(2,1)} %x.1, bf16[64,256]{1,0:T(8,128)(2,1)S(1)} %copy-done.1, bf16[32,1024]{1,0:T(8,128)(2,1)S(1)} %copy-done), custom_call_target="tpu_custom_call" | custom-call | tf_op jit(solution)/shard_map/sign_step/pallas_call | solution.py:347
  183.7 81.9 %recompress.1 = f32[48,1024]{1,0:T(8,128)} custom-call(f32[2,16,16,512]{3,2,1,0:T(8,128)S(1)} %get-tuple-element.8.aout, f32[2,16,8,768]{3,2,1,0:T(8,128)S(1)} %get-tuple-element.9.bcout, bf16[16,32,1024]{2,1,0:T(8,128)(2,1)S(1)} %get-tuple-element.10.oldall, f32[16,64,256]{2,1,0:T(8,128)S(1)} %get-tuple-element.11.pall), custom_call_target="tpu_custom_call" | custom-call | tf_op jit(solution)/shard_map/recompress/pallas_call | solution.py:390
  265.6 0.6 copy.6
Async XLA Ops:
  0.6 0.8 copy-start
  1.5 0.8 copy-start.1

commit v2 on v1

v2 whole, which is shorter than its diff:
```python
import functools

import jax
import jax.numpy as jnp
from jax import lax
from jax.experimental import pallas as pl
from jax.experimental.pallas import tpu as pltpu
from jax.sharding import PartitionSpec as P

NSTATE = 32768
MESH = pl.DeviceIdType.MESH
HIGHEST = lax.Precision.HIGHEST
BF = jnp.bfloat16
F32 = jnp.float32
NT = (((1,), (1,)), ((), ()))


def split3(a):
    hi = a.astype(BF)
    rest = a - hi.astype(F32)
    mid = rest.astype(BF)
    low = (rest - mid.astype(F32)).astype(BF)
    return hi, mid, low


def eight(g, m, out):
    n = 128
    sub = lax.broadcasted_iota(jnp.int32, (8, n), 0)
    lane = lax.broadcasted_iota(jnp.int32, (8, n), 1)
    c = [jnp.broadcast_to(m[:8, 8 + k : 9 + k], (8, n)) for k in range(8)]
    turned = pltpu.roll(m, n - 8, 1)
    top = jnp.where(lane < 8, jnp.where(lane == sub, 1.0, 0.0), turned[:8])
    lines, steps, pivots = [], [], c[0]
    for s in range(8):
        if s:
            pivots = jnp.where(sub == s, c[s], pivots)
        inv = 1.0 / c[s][s : s + 1, :]
        line = top[s : s + 1, :] * inv
        col = jnp.where(sub > s, c[s], 0.0)
        top = top - col * line
        hs = [None] * 8
        for k in range(s + 1, 8):
            hs[k] = c[k][s : s + 1, :] * inv
            c[k] = c[k] - col * hs[k]
        lines.append(line)
        steps.append(hs)
    top = top * lax.rsqrt(pivots)
    top = jnp.where((lane < 8) | (lane >= n - 8 * g), top, 0.0)
    out[pl.ds(pl.multiple_of(g * 8, 8), 8), :] = pltpu.roll(top, 8 * g, 1)
    rest = []
    for r in range(1, 16):
        cr = [jnp.broadcast_to(m[8 * r : 8 * r + 8, 8 + k : 9 + k], (8, n)) for k in range(8)]
        acc = jnp.where(lane < 8, 0.0, turned[8 * r : 8 * r + 8])
        for s in range(8):
            for k in range(s + 1, 8):
                cr[k] = cr[k] - cr[s] * steps[s][k]
            acc = acc - cr[s] * lines[s]
        rest.append(acc)
    return jnp.concatenate(rest + [jnp.zeros((8, n), F32)], 0)


def dot(a, b):
    return jnp.dot(a, b, precision=HIGHEST, preferred_element_type=F32)


def dot_nt(a, b):
    return lax.dot_general(a, b, NT, precision=HIGHEST, preferred_element_type=F32)


def factor_items(gram, inv, turning, done, blocks, pieces):
    items = []
    size = blocks * 128
    for j in range(blocks):
        lo, hi = j * 128, (j + 1) * 128
        for p in range(pieces):

            def pivots(p=p, lo=lo, hi=hi):
                m = pltpu.roll(gram[lo:hi, lo:hi], 8, 1) if p == 0 else turning[...]
                step = 16 // pieces
                m = lax.fori_loop(p * step, (p + 1) * step, lambda g, m: eight(g, m, done), m)
                if p < pieces - 1:
                    turning[...] = m

            items.append(pivots)

        def rows(lo=lo, hi=hi):
            w = done[...]
            inv[lo:hi, lo:hi] = w
            if lo:
                inv[lo:hi, 0:lo] = dot(w, inv[lo:hi, 0:lo])
            if hi < size:
                gram[hi:, lo:hi] = dot_nt(gram[hi:, lo:hi], w)

        items.append(rows)
        if hi < size:

            def below(lo=lo, hi=hi):
                factor = gram[hi:, lo:hi]
                for k in range(hi, size, 128):
                    gram[k:, k : k + 128] -= dot_nt(factor[k - hi :], factor[k - hi : k - hi + 128])
                inv[hi:, 0:hi] -= dot(factor, inv[lo:hi, 0:hi])

            items.append(below)
    return items


def comm_kernel(
    x, v, old, panel_o, oldall, pall, winv, bout, cout,
    xt, vsend, vg, part, bufr, bufl, first,
    apart, asib, ash, apl, aout, gram, turning, done,
    bpart, bsib, bs, br, bz, bsh, bfin,
    cpart, csib, cs, cr, cz, csh, cfin,
    ag_s, ag_r, fw_s, fw_r, rs_s, rs_r, og_s, og_r, pg_s, pg_r, az_s, az_r,
    a_s, a_r, b_s, b_r, c_s, c_r,
):
    row = lax.axis_index("row")
    z = lax.axis_index("col")
    chip = row // 2
    core = row % 2
    sib = (chip * 2 + 1 - core, z)
    right = (row, (z + 1) % 16)
    left = (row, (z + 15) % 16)

    def plane(d):
        y = (chip // 4 + d // 4) % 4
        w = (chip % 4 + d % 4) % 4
        return y * 4 + w

    def remote(src, dst, ssem, rsem, target):
        return pltpu.make_async_remote_copy(
            src_ref=src, dst_ref=dst, send_sem=ssem, recv_sem=rsem, device_id=target, device_id_type=MESH
        )

    barrier = pltpu.get_barrier_semaphore()

    @pl.loop(1, 16)
    def _(d):
        pl.semaphore_signal(barrier, inc=1, device_id=(plane(d) * 2 + core, z), device_id_type=MESH)
        pl.semaphore_signal(barrier, inc=1, device_id=(row, (z + d) % 16), device_id_type=MESH)

    pl.semaphore_signal(barrier, inc=1, device_id=sib, device_id_type=MESH)
    vsend[0] = v[...]
    pl.semaphore_wait(barrier, 31)

    def plane_push(src, dst, ssem, rsem):
        @pl.loop(1, 16)
        def _(d):
            remote(src, dst, ssem, rsem, (plane(d) * 2 + core, z)).start()

    def bulk(ref, ssem, rsem):
        return remote(ref.at[pl.ds(0, 15)], ref.at[pl.ds(0, 15)], ssem, rsem, sib)

    def gather_start(m):
        plane_push(vsend.at[m], vg.at[m, core * 16 + chip], ag_s.at[m], ag_r.at[m])
        vg[m, core * 16 + chip] = vsend[m]

    def product(m, half, add):
        rhs = vg[m, pl.ds(half * 16, 16)].reshape(1024, 256)
        for rb in range(2):
            lhs = xt[pl.ds(rb * 512, 512), pl.ds(pl.multiple_of(half * 1024, 1024), 1024)]
            res = jnp.dot(lhs, rhs, preferred_element_type=F32).reshape(8, 64, 256)
            if add:
                part[m, pl.ds(rb * 8, 8)] += res
            else:
                part[m, pl.ds(rb * 8, 8)] = res

    def gather_product(m):
        wait = bulk(vg.at[m], ag_s.at[m], ag_r.at[m])
        wait.wait_recv()
        span = vg.at[m, pl.ds(core * 16, 16)]
        forward = remote(span, span, fw_s.at[m], fw_r.at[m], sib)
        forward.start()
        product(m, core, False)
        forward.wait_recv()
        product(m, 1 - core, True)
        wait.wait_send()
        forward.wait_send()

    def rs_copy(m, way, s):
        buf, to = (bufr, right) if way == 0 else (bufl, left)
        dest = (z + 8 - s) % 16 if way == 0 else (z + 9 + s) % 16
        return remote(part.at[m, dest], buf.at[m, s], rs_s.at[m, way, s], rs_r.at[m, way, s], to), dest

    def reduce_scatter(m, hook):
        for way in (0, 1):
            rs_copy(m, way, 0)[0].start()
        hook(0)
        for s in range(1, 8):
            for way in (0, 1):
                if way == 1 and s == 7:
                    continue
                rs_copy(m, way, s - 1)[0].wait_recv()
                copy, dest = rs_copy(m, way, s)
                buf = bufr if way == 0 else bufl
                part[m, dest] += buf[m, s - 1]
                copy.start()
            hook(s)
        rs_copy(m, 1, 6)[0].wait_recv()
        rs_copy(m, 0, 7)[0].wait_recv()
        res = part[m, z] + bufr[m, 7] + bufl[m, 6]
        for s in range(8):
            rs_copy(m, 0, s)[0].wait_send()
            if s < 7:
                rs_copy(m, 1, s)[0].wait_send()
        return res

    def ring(own, blocks, ssem, rsem):
        def copy(way, s):
            idx = (z - s + 16) % 16 if way == 0 else (z + s) % 16
            return remote(
                own if s == 0 else blocks.at[idx], blocks.at[idx], ssem.at[way, s], rsem.at[way, s],
                right if way == 0 else left,
            )

        def step(s):
            for way in (0, 1):
                if s > 0 and not (way == 1 and s == 8):
                    copy(way, s - 1).wait_recv()
                if s < 8 and not (way == 1 and s == 7):
                    copy(way, s).start()

        def finish():
            for s in range(8):
                copy(0, s).wait_send()
                if s < 7:
                    copy(1, s).wait_send()

        return step, finish

    def total_of(parts):
        total = parts[0]
        for q in range(1, 16):
            total = total + parts[q]
        return total

    def all_sum(own, other, mine, terms, zterms, share, final, res, ssem, rsem):
        pair = remote(own.at[1 - core], other, ssem.at[0], rsem.at[0], sib)
        spread = bulk(terms, ssem.at[1], rsem.at[1])
        along = bulk(zterms, ssem.at[2], rsem.at[2])
        back = bulk(res.at[core], ssem.at[3], rsem.at[3])
        half = remote(res.at[core], res.at[core], ssem.at[4], rsem.at[4], sib)

        def to_plane():
            pair.wait_recv()
            mine[...] = own[core] + other[...]

            @pl.loop(1, 16)
            def _(d):
                q = plane(d)
                remote(mine.at[q], terms.at[chip], ssem.at[1], rsem.at[1], (q * 2 + core, z)).start()

            terms[chip] = mine[chip]

        def to_column():
            spread.wait_recv()
            share[...] = total_of(terms)

            @pl.loop(1, 16)
            def _(d):
                remote(share, zterms.at[z], ssem.at[2], rsem.at[2], (row, (z + d) % 16)).start()

            zterms[z] = share[...]

        def to_back():
            along.wait_recv()
            final[...] = total_of(zterms) * (1.0 / NSTATE)
            plane_push(final, res.at[core, chip], ssem.at[3], rsem.at[3])
            res[core, chip] = final[...]

        def to_half():
            back.wait_recv()
            half.start()

        def finish():
            half.wait_recv()
            for copy in (pair, spread, along, back, half):
                copy.wait_send()

        return pair.start, to_plane, to_column, to_back, to_half, finish

    gather_start(0)
    old_step, old_finish = ring(old, oldall, og_s, og_r)
    old_step(0)
    oldall[z] = old[...]

    @pl.loop(0, 16)
    def _(t):
        a = (t % 8) * 4 + t // 8
        both = jnp.concatenate([x[a, 0], x[a + 2, 0]], 0)
        xt[:, pl.ds(pl.multiple_of(t * 128, 128), 128)] = both.T

    old_step(1)
    old_step(2)
    gather_product(0)

    a_pair = remote(apart.at[1 - core], asib, a_s.at[0], a_r.at[0], sib)

    def hook0(s):
        if 1 <= s <= 6:
            old_step(2 + s)
        if s == 7:
            every = oldall[...].reshape(512, 1024)
            share = lax.dot_general(old[...], every, NT, preferred_element_type=F32)
            apart[...] = share.reshape(2, 16, 512)
            a_pair.start()

    first_full = reduce_scatter(0, hook0)
    first[...] = first_full
    vsend[1] = first_full.astype(BF)
    gather_start(1)
    old_finish()
    a_pair.wait_recv()
    ash[...] = apart[core] + asib[...]
    plane_push(ash, apl.at[chip], a_s.at[1], a_r.at[1])
    apl[chip] = ash[...]
    a_spread = bulk(apl, a_s.at[1], a_r.at[1])
    a_step, a_finish = ring(aout.at[core, z], aout.at[core], az_s, az_r)
    a_half = remote(aout.at[core], aout.at[core], a_s.at[2], a_r.at[2], sib)
    winv[...] = jnp.zeros((512, 512), F32)
    side = z % 2
    own_rows = lax.broadcasted_iota(jnp.int32, (128, 256), 0) // 64 == side

    def own_states(a):
        return jnp.where(own_rows, jnp.concatenate([a, a], 0), 0.0)

    gather_product(1)

    def hook1(s):
        if s == 1:
            a_spread.wait_recv()
            aout[core, z] = total_of(apl) * (1.0 / NSTATE)
        if s >= 1:
            a_step(s - 1)

    second = reduce_scatter(1, hook1)
    vsend[2] = second.astype(BF)
    gather_start(2)
    a_step(7)
    a_step(8)
    a_half.start()
    gather_product(2)

    def assemble():
        a_half.wait_recv()

        @pl.loop(0, 16)
        def _(c):
            for h in range(2):
                gram[pl.ds(pl.multiple_of(c * 32 + h * 16, 16), 16), :] = aout[h, c]

    items = [assemble] + factor_items(gram, winv, turning, done, 4, 4)

    def work(count):
        for _ in range(min(count, len(items))):
            items.pop(0)()

    b_start, b_plane, b_column, b_back, b_half, b_finish = all_sum(
        bpart, bsib, bs, br, bz, bsh, bfin, bout, b_s, b_r
    )

    def hook2(s):
        if s == 0:
            every = oldall[...].reshape(512, 1024)
            window = oldall[:, :, pl.ds(pl.multiple_of((z // 2) * 128, 128), 128)].reshape(512, 128)
            cross = jnp.zeros((512, 256), F32)
            for t in split3(part[2].reshape(1024, 256) * -0.5):
                cross = cross + jnp.dot(every, t, preferred_element_type=F32)
            for t in split3(own_states(first[...] * 1.5)):
                cross = cross + jnp.dot(window, t, preferred_element_type=F32)
            bpart[...] = cross.reshape(2, 16, 16, 256)
            b_start()
        if s == 1:
            b_plane()
        if s == 5:
            b_column()
        if s in (2, 3, 4, 6, 7):
            work(1)

    third = reduce_scatter(2, hook2)
    panel = 1.5 * first[...] - 0.5 * third
    panel_o[...] = panel
    p_step, p_finish = ring(panel_o, pall, pg_s, pg_r)
    p_step(0)
    pall[z] = panel
    turned = panel.T
    cpart[...] = dot_nt(turned, turned).reshape(2, 16, 8, 256)
    c_start, c_plane, c_column, c_back, c_half, c_finish = all_sum(
        cpart, csib, cs, cr, cz, csh, cfin, cout, c_s, c_r
    )
    c_start()
    work(1)
    c_plane()
    p_step(1)
    work(2)
    b_back()
    p_step(2)
    work(2)
    c_column()
    p_step(3)
    work(2)
    p_step(4)
    work(2)
    b_half()
    p_step(5)
    work(2)
    c_back()
    p_step(6)
    work(2)
    p_step(7)
    work(2)
    c_half()
    p_step(8)
    work(100)
    p_finish()
    a_finish()
    for copy in (a_pair, a_spread, a_half):
        copy.wait_send()
    b_finish()
    c_finish()


def basis_kernel(winv, bout, cout, oldall, pall, basis_o, gram, inv, turning, done, full):
    z = lax.axis_index("col")
    first = winv[...]
    cross = bout[...].reshape(512, 256).T
    lower = dot_nt(cross, first)
    gram[...] = cout[...].reshape(256, 256) - dot_nt(lower, lower)
    inv[...] = jnp.zeros((256, 256), F32)
    for item in factor_items(gram, inv, turning, done, 2, 1):
        item()
    last = inv[...]
    full[0:512, 0:512] = first
    full[0:512, 512:768] = jnp.zeros((512, 256), F32)
    full[512:768, 0:512] = -dot(last, dot(lower, first))
    full[512:768, 512:768] = last
    mine = full[pl.ds(pl.multiple_of(z * 48, 16), 48), :]
    every = oldall[...].reshape(512, 1024)
    res = dot_nt(mine[:, 512:], pall[...].reshape(1024, 256))
    for t in split3(mine[:, :512]):
        res = res + jnp.dot(t, every, preferred_element_type=F32)
    basis_o[...] = res


def body(iterate_t, vectors, old_factor_t):
    vm = pl.BlockSpec(memory_space=pltpu.VMEM)
    dma = pltpu.SemaphoreType.DMA
    out = jax.ShapeDtypeStruct

    def f32(*shape):
        return pltpu.VMEM(shape, F32)

    panel, oldall, pall, winv, bout, cout = pl.pallas_call(
        comm_kernel,
        out_shape=(
            out((64, 256), F32),
            out((16, 32, 1024), BF),
            out((16, 64, 256), F32),
            out((512, 512), F32),
            out((2, 16, 16, 256), F32),
            out((2, 16, 8, 256), F32),
        ),
        in_specs=[vm] * 3,
        out_specs=(vm,) * 6,
        scratch_shapes=[
            pltpu.VMEM((1024, 2048), BF),
            pltpu.VMEM((3, 64, 256), BF),
            pltpu.VMEM((3, 32, 64, 256), BF),
            f32(3, 16, 64, 256), f32(3, 8, 64, 256), f32(3, 7, 64, 256), f32(64, 256),
            f32(2, 16, 512), f32(16, 512), f32(16, 512), f32(16, 16, 512), f32(2, 16, 16, 512),
            f32(512, 512), f32(128, 128), f32(128, 128),
            f32(2, 16, 16, 256), f32(16, 16, 256), f32(16, 16, 256), f32(16, 16, 256), f32(16, 16, 256),
            f32(16, 256), f32(16, 256),
            f32(2, 16, 8, 256), f32(16, 8, 256), f32(16, 8, 256), f32(16, 8, 256), f32(16, 8, 256),
            f32(8, 256), f32(8, 256),
            dma((3,)), dma((3,)), dma((3,)), dma((3,)),
            dma((3, 2, 8)), dma((3, 2, 8)),
            dma((2, 8)), dma((2, 8)),
            dma((2, 8)), dma((2, 8)),
            dma((2, 8)), dma((2, 8)),
            dma((3,)), dma((3,)),
            dma((5,)), dma((5,)), dma((5,)), dma((5,)),
        ],
        compiler_params=pltpu.CompilerParams(
            collective_id=0, has_side_effects=True, vmem_limit_bytes=48 << 20
        ),
        name="sign_step",
    )(iterate_t, vectors, old_factor_t)
    basis = pl.pallas_call(
        basis_kernel,
        out_shape=out((48, 1024), F32),
        in_specs=[vm] * 5,
        out_specs=vm,
        scratch_shapes=[f32(256, 256), f32(256, 256), f32(128, 128), f32(128, 128), f32(768, 768)],
        compiler_params=pltpu.CompilerParams(vmem_limit_bytes=48 << 20),
        name="recompress",
    )(winv, bout, cout, oldall, pall)
    return panel, basis


def solution(mesh):
    return jax.shard_map(
        body,
        mesh=mesh,
        in_specs=(P(None, "col", None, "row"), P(("row", "col"), None), P("col", "row")),
        out_specs=(P(("row", "col"), None), P("col", "row")),
        check_vma=False,
    )
```

time: 267 us -> 201 us (0.75)
  Pallas kernels: 263 us -> 195 us
    pallas_call x1, Pallas kernels: 81.9 us -> 17 us  [body(): pl.pallas_call(basis_kernel, out_shape=out((48, 1024), F32), in_specs=[vm...]
    pallas_call x1, Pallas kernels: 182 us -> 178 us  [body(): pl.pallas_call(comm_kernel, out_shape=(out((64, 256), F32), out((16, 32,...]
where the time goes in v2:
time: 201 us; the launch traced here: 198 us
  Pallas kernels  195 us (97%)
  local copies, waits for them, and re-layouts  2.22 us (1%)
    pallas_call x1, Pallas kernels, body(): pl.pallas_call(comm_kernel, out_shape=(out((64, 256), F32), out((16, 32,...  178 us
    pallas_call x1, Pallas kernels, body(): pl.pallas_call(basis_kernel, out_shape=out((48, 1024), F32), in_specs=[vm...  17 us

profile of v2, /device:TPU:1, one launch (start us, length us, event | category | flops | bytes accessed | tf_op | source)
XLA Modules:
  0.0 198.0 jit_solution(15926077902373255422)
XLA Ops:
  0.6 0.0 copy-start
  0.6 0.8 copy-done
  1.5 0.0 copy-start.1
  1.5 0.8 copy-done.1
  2.2 178.2 %sign_step.1 = (f32[64,256]{1,0:T(8,128)S(1)}, bf16[16,32,1024]{2,1,0:T(8,128)(2,1)S(1)}, f32[16,64,256]{2,1,0:T(8,128)S(1)}, f32[512,512]{1,0:T(8,128)S(1)}, f3...) custom-call(bf16[32,1,64,1024]{3,2,1,0:T(8,128)(2,1)} %x.1, bf16[64,256]{1,0:T(8,128)(2,1)S(1)} %copy-done.1, ...), custom_call_target="tpu_custom_call" | custom-call | tf_op jit(solution)/shard_map/sign_step/pallas_call | solution.py:452
  180.4 17.0 %recompress.1 = f32[48,1024]{1,0:T(8,128)} custom-call(f32[512,512]{1,0:T(8,128)S(1)} %get-tuple-element.9.winv, f32[2,16,16,256]{3,2,1,0:T(8,128)S(1)} %get-tuple-element.10.bout, f32[2,16,8,256]{3,2,1,0:T(8,128)S(1)} %get-tuple-element.11.cout, bf16[16,32,1024]{2,1,0:T(8,128)(2,1)S(1)} %get-tuple-element.12.oldall, f32[16,64,256]{2,1,0:T(8,128)S(1)} %get-tuple-element.13.pall), custom_call_target="tpu_custom_call" | custom-call | tf_op jit(solution)/shard_map/recompress/pallas_call | solution.py:488
  197.4 0.6 copy.6
Async XLA Ops:
  0.6 0.8 copy-start
  1.5 0.8 copy-start.1

commit v3 on v2

--- a/solution.py
+++ b/solution.py
@@ -89,27 +89,28 @@
             if lo:
                 inv[lo:hi, 0:lo] = dot(w, inv[lo:hi, 0:lo])
             if hi < size:
-                gram[hi:, lo:hi] = dot_nt(gram[hi:, lo:hi], w)
+                gram[hi:size, lo:hi] = dot_nt(gram[hi:size, lo:hi], w)
 
         items.append(rows)
         if hi < size:
 
             def below(lo=lo, hi=hi):
-                factor = gram[hi:, lo:hi]
+                factor = gram[hi:size, lo:hi]
                 for k in range(hi, size, 128):
-                    gram[k:, k : k + 128] -= dot_nt(factor[k - hi :], factor[k - hi : k - hi + 128])
-                inv[hi:, 0:hi] -= dot(factor, inv[lo:hi, 0:hi])
+                    gram[k:size, k : k + 128] -= dot_nt(factor[k - hi :], factor[k - hi : k - hi + 128])
+                inv[hi:size, 0:hi] -= dot(factor, inv[lo:hi, 0:hi])
 
             items.append(below)
     return items
 
 
 def comm_kernel(
-    x, v, old, panel_o, oldall, pall, winv, bout, cout,
-    xt, vsend, vg, part, bufr, bufl, first,
-    apart, asib, ash, apl, aout, gram, turning, done,
-    bpart, bsib, bs, br, bz, bsh, bfin,
-    cpart, csib, cs, cr, cz, csh, cfin,
+    x, v, old, panel_o, basis_o,
+    xs, xt, vsend, vg, part, meet, hub_sum, landed, first, oldall, pall,
+    apart, asib, ash, apl, aout, gram, turning, done, winv,
+    bsplit, bpart, bsib, bs, br, bz, bsh, bfin, bout,
+    cpart, csib, cs, cr, cz, csh, cfin, cout,
+    lower, onto, square, gram2, inv2, upper, tmat, x_s,
     ag_s, ag_r, fw_s, fw_r, rs_s, rs_r, og_s, og_r, pg_s, pg_r, az_s, az_r,
     a_s, a_r, b_s, b_r, c_s, c_r,
 ):
@@ -131,6 +132,11 @@
             src_ref=src, dst_ref=dst, send_sem=ssem, recv_sem=rsem, device_id=target, device_id_type=MESH
         )
 
+    loads = [
+        pltpu.make_async_copy(x.at[pl.ds(8 * q, 8), 0], xs.at[pl.ds(8 * q, 8)], x_s.at[q]) for q in range(4)
+    ]
+    for load in loads:
+        load.start()
     barrier = pltpu.get_barrier_semaphore()
 
     @pl.loop(1, 16)
@@ -140,6 +146,17 @@
 
     pl.semaphore_signal(barrier, inc=1, device_id=sib, device_id_type=MESH)
     vsend[0] = v[...]
+
+    for q in range(4):
+        loads[q].wait()
+
+        @pl.loop(0, 4)
+        def _(u):
+            a = 8 * q + (u // 2) * 4 + u % 2
+            at = ((u % 2) * 8 + 2 * q + u // 2) * 128
+            both = jnp.concatenate([xs[a], xs[a + 2]], 0)
+            xt[:, pl.ds(pl.multiple_of(at, 128), 128)] = both.T
+
     pl.semaphore_wait(barrier, 31)
 
     def plane_push(src, dst, ssem, rsem):
@@ -176,32 +193,46 @@
         wait.wait_send()
         forward.wait_send()
 
-    def rs_copy(m, way, s):
-        buf, to = (bufr, right) if way == 0 else (bufl, left)
-        dest = (z + 8 - s) % 16 if way == 0 else (z + 9 + s) % 16
-        return remote(part.at[m, dest], buf.at[m, s], rs_s.at[m, way, s], rs_r.at[m, way, s], to), dest
-
-    def reduce_scatter(m, hook):
-        for way in (0, 1):
-            rs_copy(m, way, 0)[0].start()
-        hook(0)
-        for s in range(1, 8):
-            for way in (0, 1):
-                if way == 1 and s == 7:
-                    continue
-                rs_copy(m, way, s - 1)[0].wait_recv()
-                copy, dest = rs_copy(m, way, s)
-                buf = bufr if way == 0 else bufl
-                part[m, dest] += buf[m, s - 1]
-                copy.start()
-            hook(s)
-        rs_copy(m, 1, 6)[0].wait_recv()
-        rs_copy(m, 0, 7)[0].wait_recv()
-        res = part[m, z] + bufr[m, 7] + bufl[m, 6]
-        for s in range(8):
-            rs_copy(m, 0, s)[0].wait_send()
-            if s < 7:
-                rs_copy(m, 1, s)[0].wait_send()
+    def at(d):
+        return (z + 16 + d) % 16
+
+    def flight(m, slot, hub, dest, sem):
+        return remote(part.at[m, at(dest)], meet.at[m, slot], rs_s.at[m, 0], rs_r.at[m, sem], (row, at(hub)))
+
+    def reduce_scatter(m, early, late):
+        for i, d in enumerate((3, 2, -2, 1, -1)):
+            flight(m, i, -d, -d - 5, 0).start()
+        for i, d in enumerate((2, -2, 1, -1)):
+            flight(m, 5 + i, -d, -d + 5, 1).start()
+        for i, d in enumerate((2, -2, 1, -1)):
+            flight(m, 9 + i, -d, -d, 2).start()
+
+        def met(first, count, sem):
+            span = meet.at[m, pl.ds(first, count)]
+            remote(span, span, rs_s.at[m, 0], rs_r.at[m, sem], sib).wait_recv()
+            total = meet[m, first]
+            for k in range(first + 1, first + count):
+                total = total + meet[m, k]
+            return total
+
+        early()
+        onward = []
+        for k, (first, count, dest) in enumerate(((0, 5, -5), (5, 4, 5))):
+            hub_sum[m, k] = part[m, at(dest)] + met(first, count, k)
+            copy = remote(
+                hub_sum.at[m, k], landed.at[m, k], rs_s.at[m, 1 + k], rs_r.at[m, 3 + k], (row, at(dest))
+            )
+            copy.start()
+            onward.append(copy)
+        near = part[m, z] + met(9, 4, 2)
+        late()
+        for copy in onward:
+            copy.wait_recv()
+        res = near + (landed[m, 0] + landed[m, 1])
+        span = meet.at[m, pl.ds(0, 13)]
+        remote(span, span, rs_s.at[m, 0], rs_r.at[m, 0], sib).wait_send()
+        for copy in onward:
+            copy.wait_send()
         return res
 
     def ring(own, blocks, ssem, rsem):
@@ -272,73 +303,75 @@
             half.start()
 
         def finish():
-            half.wait_recv()
             for copy in (pair, spread, along, back, half):
                 copy.wait_send()
 
-        return pair.start, to_plane, to_column, to_back, to_half, finish
+        return pair.start, to_plane, to_column, to_back, to_half, half.wait_recv, finish
 
     gather_start(0)
     old_step, old_finish = ring(old, oldall, og_s, og_r)
     old_step(0)
     oldall[z] = old[...]
 
-    @pl.loop(0, 16)
-    def _(t):
-        a = (t % 8) * 4 + t // 8
-        both = jnp.concatenate([x[a, 0], x[a + 2, 0]], 0)
-        xt[:, pl.ds(pl.multiple_of(t * 128, 128), 128)] = both.T
-
     old_step(1)
     old_step(2)
+    old_step(3)
     gather_product(0)
 
     a_pair = remote(apart.at[1 - core], asib, a_s.at[0], a_r.at[0], sib)
-
-    def hook0(s):
-        if 1 <= s <= 6:
-            old_step(2 + s)
-        if s == 7:
-            every = oldall[...].reshape(512, 1024)
-            share = lax.dot_general(old[...], every, NT, preferred_element_type=F32)
-            apart[...] = share.reshape(2, 16, 512)
-            a_pair.start()
-
-    first_full = reduce_scatter(0, hook0)
+    a_spread = bulk(apl, a_s.at[1], a_r.at[1])
+
+    def early0():
+        for s in (4, 5, 6):
+            old_step(s)
+
+    def late0():
+        old_step(7)
+        old_step(8)
+        every = oldall[...].reshape(512, 1024)
+        share = lax.dot_general(old[...], every, NT, preferred_element_type=F32)
+        apart[...] = share.reshape(2, 16, 512)
+        a_pair.start()
+
+    first_full = reduce_scatter(0, early0, late0)
     first[...] = first_full
     vsend[1] = first_full.astype(BF)
     gather_start(1)
-    old_finish()
     a_pair.wait_recv()
     ash[...] = apart[core] + asib[...]
     plane_push(ash, apl.at[chip], a_s.at[1], a_r.at[1])
     apl[chip] = ash[...]
-    a_spread = bulk(apl, a_s.at[1], a_r.at[1])
+    old_finish()
     a_step, a_finish = ring(aout.at[core, z], aout.at[core], az_s, az_r)
     a_half = remote(aout.at[core], aout.at[core], a_s.at[2], a_r.at[2], sib)
-    winv[...] = jnp.zeros((512, 512), F32)
+    winv[...] = jnp.zeros((768, 512), F32)
+    upper[...] = jnp.zeros((768, 256), F32)
+    inv2[...] = jnp.zeros((256, 256), F32)
     side = z % 2
     own_rows = lax.broadcasted_iota(jnp.int32, (128, 256), 0) // 64 == side
 
     def own_states(a):
         return jnp.where(own_rows, jnp.concatenate([a, a], 0), 0.0)
 
+    a_spread.wait_recv()
+    aout[core, z] = total_of(apl) * (1.0 / NSTATE)
+    a_step(0)
+    a_step(1)
     gather_product(1)
 
-    def hook1(s):
-        if s == 1:
-            a_spread.wait_recv()
-            aout[core, z] = total_of(apl) * (1.0 / NSTATE)
-        if s >= 1:
-            a_step(s - 1)
-
-    second = reduce_scatter(1, hook1)
+    def early1():
+        for s in (2, 3, 4):
+            a_step(s)
+
+    def late1():
+        for s in (5, 6, 7):
+            a_step(s)
+
+    second = reduce_scatter(1, early1, late1)
     vsend[2] = second.astype(BF)
     gather_start(2)
-    a_step(7)
     a_step(8)
     a_half.start()
-    gather_product(2)
 
     def assemble():
         a_half.wait_recv()
@@ -354,63 +387,97 @@
         for _ in range(min(count, len(items))):
             items.pop(0)()
 
-    b_start, b_plane, b_column, b_back, b_half, b_finish = all_sum(
+    work(6)
+    gather_product(2)
+    b_start, b_plane, b_column, b_back, b_half, b_ready, b_finish = all_sum(
         bpart, bsib, bs, br, bz, bsh, bfin, bout, b_s, b_r
     )
 
-    def hook2(s):
-        if s == 0:
-            every = oldall[...].reshape(512, 1024)
-            window = oldall[:, :, pl.ds(pl.multiple_of((z // 2) * 128, 128), 128)].reshape(512, 128)
-            cross = jnp.zeros((512, 256), F32)
-            for t in split3(part[2].reshape(1024, 256) * -0.5):
-                cross = cross + jnp.dot(every, t, preferred_element_type=F32)
-            for t in split3(own_states(first[...] * 1.5)):
-                cross = cross + jnp.dot(window, t, preferred_element_type=F32)
-            bpart[...] = cross.reshape(2, 16, 16, 256)
-            b_start()
-        if s == 1:
-            b_plane()
-        if s == 5:
-            b_column()
-        if s in (2, 3, 4, 6, 7):
-            work(1)
-
-    third = reduce_scatter(2, hook2)
+    def every_old():
+        return oldall[...].reshape(512, 1024)
+
+    def early2():
+        for t, piece in enumerate(split3(part[2].reshape(1024, 256) * -0.5)):
+            bsplit[t] = piece
+        cross = jnp.zeros((512, 256), F32)
+        for t in range(3):
+            cross = cross + jnp.dot(every_old(), bsplit[t], preferred_element_type=F32)
+        window = oldall[:, :, pl.ds(pl.multiple_of((z // 2) * 128, 128), 128)].reshape(512, 128)
+        for t in split3(own_states(first[...] * 1.5)):
+            cross = cross + jnp.dot(window, t, preferred_element_type=F32)
+        bpart[...] = cross.reshape(2, 16, 16, 256)
+        b_start()
+        work(1)
+
+    def late2():
+        b_plane()
+        work(4)
+
+    third = reduce_scatter(2, early2, late2)
     panel = 1.5 * first[...] - 0.5 * third
     panel_o[...] = panel
     p_step, p_finish = ring(panel_o, pall, pg_s, pg_r)
-    p_step(0)
-    pall[z] = panel
     turned = panel.T
     cpart[...] = dot_nt(turned, turned).reshape(2, 16, 8, 256)
-    c_start, c_plane, c_column, c_back, c_half, c_finish = all_sum(
+    c_start, c_plane, c_column, c_back, c_half, c_ready, c_finish = all_sum(
         cpart, csib, cs, cr, cz, csh, cfin, cout, c_s, c_r
     )
     c_start()
-    work(1)
+    p_step(0)
+    pall[z] = panel
     c_plane()
+    b_column()
+
+    def to_lower():
+        b_ready()
+        lower[...] = dot_nt(bout[...].reshape(512, 256).T, winv[0:512, :])
+
+    def to_square():
+        square[...] = dot_nt(lower[...], lower[...])
+
+    def to_onto():
+        onto[...] = dot(lower[...], winv[0:512, :])
+
+    def to_old_rows():
+        res = jnp.zeros((48, 1024), F32)
+        for t in split3(winv[pl.ds(pl.multiple_of(z * 48, 16), 48), :]):
+            res = res + jnp.dot(t, every_old(), preferred_element_type=F32)
+        basis_o[...] = res
+
+    def to_rest():
+        res = pall[...].reshape(1024, 256).T
+        for t in split3(onto[...]):
+            res = res - jnp.dot(t, every_old(), preferred_element_type=F32)
+        tmat[...] = res
+
+    items.extend([to_lower, to_square, to_onto, to_old_rows])
     p_step(1)
-    work(2)
+    work(3)
+    c_column()
     b_back()
     p_step(2)
     work(2)
-    c_column()
     p_step(3)
     work(2)
+    b_half()
     p_step(4)
     work(2)
-    b_half()
+    c_back()
     p_step(5)
     work(2)
-    c_back()
     p_step(6)
-    work(2)
+    work(1)
+    c_half()
     p_step(7)
-    work(2)
-    c_half()
+    work(100)
     p_step(8)
-    work(100)
+    to_rest()
+    c_ready()
+    gram2[...] = cout[...].reshape(256, 256) - square[...]
+    for item in factor_items(gram2, inv2, turning, done, 2, 1):
+        item()
+    upper[512:768, :] = inv2[...]
+    basis_o[...] += dot(upper[pl.ds(pl.multiple_of(z * 48, 16), 48), :], tmat[...])
     p_finish()
     a_finish()
     for copy in (a_pair, a_spread, a_half):
@@ -419,28 +486,6 @@
     c_finish()
 
 
-def basis_kernel(winv, bout, cout, oldall, pall, basis_o, gram, inv, turning, done, full):
-    z = lax.axis_index("col")
-    first = winv[...]
-    cross = bout[...].reshape(512, 256).T
-    lower = dot_nt(cross, first)
-    gram[...] = cout[...].reshape(256, 256) - dot_nt(lower, lower)
-    inv[...] = jnp.zeros((256, 256), F32)
-    for item in factor_items(gram, inv, turning, done, 2, 1):
-        item()
-    last = inv[...]
-    full[0:512, 0:512] = first
-    full[0:512, 512:768] = jnp.zeros((512, 256), F32)
-    full[512:768, 0:512] = -dot(last, dot(lower, first))
-    full[512:768, 512:768] = last
-    mine = full[pl.ds(pl.multiple_of(z * 48, 16), 48), :]
-    every = oldall[...].reshape(512, 1024)
-    res = dot_nt(mine[:, 512:], pall[...].reshape(1024, 256))
-    for t in split3(mine[:, :512]):
-        res = res + jnp.dot(t, every, preferred_element_type=F32)
-    basis_o[...] = res
-
-
 def body(iterate_t, vectors, old_factor_t):
     vm = pl.BlockSpec(memory_space=pltpu.VMEM)
     dma = pltpu.SemaphoreType.DMA
@@ -449,31 +494,29 @@
     def f32(*shape):
         return pltpu.VMEM(shape, F32)
 
-    panel, oldall, pall, winv, bout, cout = pl.pallas_call(
+    return pl.pallas_call(
         comm_kernel,
-        out_shape=(
-            out((64, 256), F32),
-            out((16, 32, 1024), BF),
-            out((16, 64, 256), F32),
-            out((512, 512), F32),
-            out((2, 16, 16, 256), F32),
-            out((2, 16, 8, 256), F32),
-        ),
-        in_specs=[vm] * 3,
-        out_specs=(vm,) * 6,
+        out_shape=(out((64, 256), F32), out((48, 1024), F32)),
+        in_specs=[pl.BlockSpec(memory_space=pl.ANY), vm, vm],
+        out_specs=(vm, vm),
         scratch_shapes=[
+            pltpu.VMEM((32, 64, 1024), BF),
             pltpu.VMEM((1024, 2048), BF),
             pltpu.VMEM((3, 64, 256), BF),
             pltpu.VMEM((3, 32, 64, 256), BF),
-            f32(3, 16, 64, 256), f32(3, 8, 64, 256), f32(3, 7, 64, 256), f32(64, 256),
+            f32(3, 16, 64, 256), f32(3, 13, 64, 256), f32(3, 2, 64, 256), f32(3, 2, 64, 256), f32(64, 256),
+            pltpu.VMEM((16, 32, 1024), BF), f32(16, 64, 256),
             f32(2, 16, 512), f32(16, 512), f32(16, 512), f32(16, 16, 512), f32(2, 16, 16, 512),
-            f32(512, 512), f32(128, 128), f32(128, 128),
+            f32(512, 512), f32(128, 128), f32(128, 128), f32(768, 512),
+            pltpu.VMEM((3, 1024, 256), BF),
             f32(2, 16, 16, 256), f32(16, 16, 256), f32(16, 16, 256), f32(16, 16, 256), f32(16, 16, 256),
-            f32(16, 256), f32(16, 256),
+            f32(16, 256), f32(16, 256), f32(2, 16, 16, 256),
             f32(2, 16, 8, 256), f32(16, 8, 256), f32(16, 8, 256), f32(16, 8, 256), f32(16, 8, 256),
-            f32(8, 256), f32(8, 256),
+            f32(8, 256), f32(8, 256), f32(2, 16, 8, 256),
+            f32(256, 512), f32(256, 512), f32(256, 256), f32(256, 256), f32(256, 256), f32(768, 256),
+            f32(256, 1024), dma((4,)),
             dma((3,)), dma((3,)), dma((3,)), dma((3,)),
-            dma((3, 2, 8)), dma((3, 2, 8)),
+            dma((3, 3)), dma((3, 5)),
             dma((2, 8)), dma((2, 8)),
             dma((2, 8)), dma((2, 8)),
             dma((2, 8)), dma((2, 8)),
@@ -481,20 +524,10 @@
             dma((5,)), dma((5,)), dma((5,)), dma((5,)),
         ],
         compiler_params=pltpu.CompilerParams(
-            collective_id=0, has_side_effects=True, vmem_limit_bytes=48 << 20
+            collective_id=0, has_side_effects=True, vmem_limit_bytes=56 << 20
         ),
         name="sign_step",
     )(iterate_t, vectors, old_factor_t)
-    basis = pl.pallas_call(
-        basis_kernel,
-        out_shape=out((48, 1024), F32),
-        in_specs=[vm] * 5,
-        out_specs=vm,
-        scratch_shapes=[f32(256, 256), f32(256, 256), f32(128, 128), f32(128, 128), f32(768, 768)],
-        compiler_params=pltpu.CompilerParams(vmem_limit_bytes=48 << 20),
-        name="recompress",
-    )(winv, bout, cout, oldall, pall)
-    return panel, basis
 
 
 def solution(mesh):

time: 201 us -> 221 us (1.100)
  Pallas kernels: 195 us -> 214 us
    pallas_call x2 -> x1, Pallas kernels: 195 us -> 214 us  [body(): pl.pallas_call(comm_kernel, out_shape=(out((64, 256), F32), out((48, 1024...]
where the time goes in v3:
time: 221 us; the launch traced here: 218 us
  Pallas kernels  214 us (97%)
  local copies, waits for them, and re-layouts  3.09 us (1%)
    pallas_call x1, Pallas kernels, body(): pl.pallas_call(comm_kernel, out_shape=(out((64, 256), F32), out((48, 1024...  214 us

profile of v3, /device:TPU:1, one launch (start us, length us, event | category | flops | bytes accessed | tf_op | source)
XLA Modules:
  0.0 218.1 jit_solution(4170523198007138686)
XLA Ops:
  0.6 214.4 %sign_step.1 = (f32[64,256]{1,0:T(8,128)}, f32[48,1024]{1,0:T(8,128)}) custom-call(bf16[32,1,64,1024]{3,2,1,0:T(8,128)(2,1)} %x.1, bf16[64,256]{1,0:T(8,128)(2,1)} %v.1, bf16[32,1024]{1,0:T(8,128)(2,1)} %old.1), custom_call_target="tpu_custom_call" | custom-call | tf_op jit(solution)/shard_map/sign_step/pallas_call | solution.py:497
  215.0 1.5 copy.7
  216.5 1.6 copy.8

commit v4 on v3

--- a/solution.py
+++ b/solution.py
@@ -106,12 +106,12 @@
 
 def comm_kernel(
     x, v, old, panel_o, basis_o,
-    xs, xt, vsend, vg, part, meet, hub_sum, landed, first, oldall, pall,
-    apart, asib, ash, apl, aout, gram, turning, done, winv,
-    bsplit, bpart, bsib, bs, br, bz, bsh, bfin, bout,
+    xs, xt, vsend, vg, part, bufr, bufl, first, oldall, pall,
+    apart, asib, ash, apl, afin, aout, gram, turning, done, winv,
+    bsplit, bacc, bpart, bsib, bs, br, bz, bsh, bfin, bout,
     cpart, csib, cs, cr, cz, csh, cfin, cout,
     lower, onto, square, gram2, inv2, upper, tmat, x_s,
-    ag_s, ag_r, fw_s, fw_r, rs_s, rs_r, og_s, og_r, pg_s, pg_r, az_s, az_r,
+    ag_s, ag_r, fw_s, fw_r, rs_s, rs_r, og_s, og_r, pg_s, pg_r,
     a_s, a_r, b_s, b_r, c_s, c_r,
 ):
     row = lax.axis_index("row")
@@ -168,7 +168,10 @@
         return remote(ref.at[pl.ds(0, 15)], ref.at[pl.ds(0, 15)], ssem, rsem, sib)
 
     def gather_start(m):
-        plane_push(vsend.at[m], vg.at[m, core * 16 + chip], ag_s.at[m], ag_r.at[m])
+        for d in (10, 9, 11, 6, 14, 2, 8, 5, 7, 13, 15, 1, 3, 4, 12):
+            remote(
+                vsend.at[m], vg.at[m, core * 16 + chip], ag_s.at[m], ag_r.at[m], (plane(d) * 2 + core, z)
+            ).start()
         vg[m, core * 16 + chip] = vsend[m]
 
     def product(m, half, add):
@@ -193,46 +196,39 @@
         wait.wait_send()
         forward.wait_send()
 
-    def at(d):
-        return (z + 16 + d) % 16
-
-    def flight(m, slot, hub, dest, sem):
-        return remote(part.at[m, at(dest)], meet.at[m, slot], rs_s.at[m, 0], rs_r.at[m, sem], (row, at(hub)))
-
-    def reduce_scatter(m, early, late):
-        for i, d in enumerate((3, 2, -2, 1, -1)):
-            flight(m, i, -d, -d - 5, 0).start()
-        for i, d in enumerate((2, -2, 1, -1)):
-            flight(m, 5 + i, -d, -d + 5, 1).start()
-        for i, d in enumerate((2, -2, 1, -1)):
-            flight(m, 9 + i, -d, -d, 2).start()
-
-        def met(first, count, sem):
-            span = meet.at[m, pl.ds(first, count)]
-            remote(span, span, rs_s.at[m, 0], rs_r.at[m, sem], sib).wait_recv()
-            total = meet[m, first]
-            for k in range(first + 1, first + count):
-                total = total + meet[m, k]
-            return total
-
-        early()
-        onward = []
-        for k, (first, count, dest) in enumerate(((0, 5, -5), (5, 4, 5))):
-            hub_sum[m, k] = part[m, at(dest)] + met(first, count, k)
-            copy = remote(
-                hub_sum.at[m, k], landed.at[m, k], rs_s.at[m, 1 + k], rs_r.at[m, 3 + k], (row, at(dest))
-            )
-            copy.start()
-            onward.append(copy)
-        near = part[m, z] + met(9, 4, 2)
-        late()
-        for copy in onward:
-            copy.wait_recv()
-        res = near + (landed[m, 0] + landed[m, 1])
-        span = meet.at[m, pl.ds(0, 13)]
-        remote(span, span, rs_s.at[m, 0], rs_r.at[m, 0], sib).wait_send()
-        for copy in onward:
-            copy.wait_send()
+    def rs_copy(m, way, s, h):
+        buf, to = (bufr, right) if way == 0 else (bufl, left)
+        dest = (z + 8 - s) % 16 if way == 0 else (z + 9 + s) % 16
+        rows = pl.ds(h * 32, 32)
+        return remote(
+            part.at[m, dest, rows], buf.at[m, s, rows], rs_s.at[m, way, s, h], rs_r.at[m, way, s, h], to
+        ), dest
+
+    def reduce_scatter(m, hook):
+        for h in (0, 1):
+            for way in (0, 1):
+                rs_copy(m, way, 0, h)[0].start()
+        hook(0)
+        for s in range(1, 8):
+            for h in (0, 1):
+                for way in (0, 1):
+                    if way == 1 and s == 7:
+                        continue
+                    rs_copy(m, way, s - 1, h)[0].wait_recv()
+                    copy, dest = rs_copy(m, way, s, h)
+                    rows = pl.ds(h * 32, 32)
+                    part[m, dest, rows] += (bufr if way == 0 else bufl)[m, s - 1, rows]
+                    copy.start()
+            hook(s)
+        for h in (0, 1):
+            rs_copy(m, 1, 6, h)[0].wait_recv()
+            rs_copy(m, 0, 7, h)[0].wait_recv()
+        res = part[m, z] + bufr[m, 7] + bufl[m, 6]
+        for h in (0, 1):
+            for s in range(8):
+                rs_copy(m, 0, s, h)[0].wait_send()
+                if s < 7:
+                    rs_copy(m, 1, s, h)[0].wait_send()
         return res
 
     def ring(own, blocks, ssem, rsem):
@@ -267,7 +263,7 @@
     def all_sum(own, other, mine, terms, zterms, share, final, res, ssem, rsem):
         pair = remote(own.at[1 - core], other, ssem.at[0], rsem.at[0], sib)
         spread = bulk(terms, ssem.at[1], rsem.at[1])
-        along = bulk(zterms, ssem.at[2], rsem.at[2])
+        along = None if zterms is None else bulk(zterms, ssem.at[2], rsem.at[2])
         back = bulk(res.at[core], ssem.at[3], rsem.at[3])
         half = remote(res.at[core], res.at[core], ssem.at[4], rsem.at[4], sib)
 
@@ -284,6 +280,10 @@
 
         def to_column():
             spread.wait_recv()
+            if along is None:
+                final[...] = total_of(terms) * (1.0 / NSTATE)
+                send_back()
+                return
             share[...] = total_of(terms)
 
             @pl.loop(1, 16)
@@ -292,18 +292,21 @@
 
             zterms[z] = share[...]
 
+        def send_back():
+            plane_push(final, res.at[core, chip], ssem.at[3], rsem.at[3])
+            res[core, chip] = final[...]
+
         def to_back():
             along.wait_recv()
             final[...] = total_of(zterms) * (1.0 / NSTATE)
-            plane_push(final, res.at[core, chip], ssem.at[3], rsem.at[3])
-            res[core, chip] = final[...]
+            send_back()
 
         def to_half():
             back.wait_recv()
             half.start()
 
         def finish():
-            for copy in (pair, spread, along, back, half):
+            for copy in [pair, spread, back, half] + ([] if along is None else [along]):
                 copy.wait_send()
 
         return pair.start, to_plane, to_column, to_back, to_half, half.wait_recv, finish
@@ -316,34 +319,30 @@
     old_step(1)
     old_step(2)
     old_step(3)
+    old_step(4)
     gather_product(0)
 
-    a_pair = remote(apart.at[1 - core], asib, a_s.at[0], a_r.at[0], sib)
-    a_spread = bulk(apl, a_s.at[1], a_r.at[1])
-
-    def early0():
-        for s in (4, 5, 6):
-            old_step(s)
-
-    def late0():
-        old_step(7)
-        old_step(8)
-        every = oldall[...].reshape(512, 1024)
-        share = lax.dot_general(old[...], every, NT, preferred_element_type=F32)
-        apart[...] = share.reshape(2, 16, 512)
-        a_pair.start()
-
-    first_full = reduce_scatter(0, early0, late0)
+    a_start, a_plane, a_back, _, a_half, a_ready, a_finish = all_sum(
+        apart, asib, ash, apl, None, None, afin, aout, a_s, a_r
+    )
+
+    def hook0(s):
+        if 1 <= s <= 4:
+            old_step(4 + s)
+        if s == 5:
+            every = oldall[...].reshape(512, 1024)
+            for h in range(2):
+                share = lax.dot_general(every[h * 256 : h * 256 + 256], every, NT, preferred_element_type=F32)
+                apart[h] = share.reshape(16, 16, 512)
+            a_start()
+        if s == 6:
+            a_plane()
+
+    first_full = reduce_scatter(0, hook0)
     first[...] = first_full
     vsend[1] = first_full.astype(BF)
     gather_start(1)
-    a_pair.wait_recv()
-    ash[...] = apart[core] + asib[...]
-    plane_push(ash, apl.at[chip], a_s.at[1], a_r.at[1])
-    apl[chip] = ash[...]
     old_finish()
-    a_step, a_finish = ring(aout.at[core, z], aout.at[core], az_s, az_r)
-    a_half = remote(aout.at[core], aout.at[core], a_s.at[2], a_r.at[2], sib)
     winv[...] = jnp.zeros((768, 512), F32)
     upper[...] = jnp.zeros((768, 256), F32)
     inv2[...] = jnp.zeros((256, 256), F32)
@@ -353,33 +352,11 @@
     def own_states(a):
         return jnp.where(own_rows, jnp.concatenate([a, a], 0), 0.0)
 
-    a_spread.wait_recv()
-    aout[core, z] = total_of(apl) * (1.0 / NSTATE)
-    a_step(0)
-    a_step(1)
     gather_product(1)
 
-    def early1():
-        for s in (2, 3, 4):
-            a_step(s)
-
-    def late1():
-        for s in (5, 6, 7):
-            a_step(s)
-
-    second = reduce_scatter(1, early1, late1)
-    vsend[2] = second.astype(BF)
-    gather_start(2)
-    a_step(8)
-    a_half.start()
-
     def assemble():
-        a_half.wait_recv()
-
-        @pl.loop(0, 16)
-        def _(c):
-            for h in range(2):
-                gram[pl.ds(pl.multiple_of(c * 32 + h * 16, 16), 16), :] = aout[h, c]
+        a_ready()
+        gram[...] = aout[...].reshape(512, 512)
 
     items = [assemble] + factor_items(gram, winv, turning, done, 4, 4)
 
@@ -387,7 +364,19 @@
         for _ in range(min(count, len(items))):
             items.pop(0)()
 
-    work(6)
+    def hook1(s):
+        if s == 1:
+            a_back()
+        if s == 5:
+            a_half()
+        if s == 7:
+            work(2)
+
+    second = reduce_scatter(1, hook1)
+    vsend[2] = second.astype(BF)
+    gather_start(2)
+
+    work(8)
     gather_product(2)
     b_start, b_plane, b_column, b_back, b_half, b_ready, b_finish = all_sum(
         bpart, bsib, bs, br, bz, bsh, bfin, bout, b_s, b_r
@@ -396,24 +385,28 @@
     def every_old():
         return oldall[...].reshape(512, 1024)
 
-    def early2():
-        for t, piece in enumerate(split3(part[2].reshape(1024, 256) * -0.5)):
-            bsplit[t] = piece
-        cross = jnp.zeros((512, 256), F32)
-        for t in range(3):
-            cross = cross + jnp.dot(every_old(), bsplit[t], preferred_element_type=F32)
-        window = oldall[:, :, pl.ds(pl.multiple_of((z // 2) * 128, 128), 128)].reshape(512, 128)
-        for t in split3(own_states(first[...] * 1.5)):
-            cross = cross + jnp.dot(window, t, preferred_element_type=F32)
-        bpart[...] = cross.reshape(2, 16, 16, 256)
-        b_start()
-        work(1)
-
-    def late2():
-        b_plane()
-        work(4)
-
-    third = reduce_scatter(2, early2, late2)
+    def hook2(s):
+        if s == 0:
+            for t, piece in enumerate(split3(part[2].reshape(1024, 256) * -0.5)):
+                bsplit[t] = piece
+        if s <= 2:
+            term = jnp.dot(every_old(), bsplit[s], preferred_element_type=F32)
+            bacc[...] = term if s == 0 else bacc[...] + term
+        if s == 2:
+            cross = bacc[...]
+            window = oldall[:, :, pl.ds(pl.multiple_of((z // 2) * 128, 128), 128)].reshape(512, 128)
+            for t in split3(own_states(first[...] * 1.5)):
+                cross = cross + jnp.dot(window, t, preferred_element_type=F32)
+            bpart[...] = cross.reshape(2, 16, 16, 256)
+            b_start()
+        if s == 3:
+            b_plane()
+        if s == 6:
+            b_column()
+        if s in (4, 5, 7):
+            work(1)
+
+    third = reduce_scatter(2, hook2)
     panel = 1.5 * first[...] - 0.5 * third
     panel_o[...] = panel
     p_step, p_finish = ring(panel_o, pall, pg_s, pg_r)
@@ -426,7 +419,6 @@
     p_step(0)
     pall[z] = panel
     c_plane()
-    b_column()
 
     def to_lower():
         b_ready()
@@ -451,15 +443,15 @@
         tmat[...] = res
 
     items.extend([to_lower, to_square, to_onto, to_old_rows])
+    b_back()
     p_step(1)
     work(3)
     c_column()
-    b_back()
     p_step(2)
     work(2)
+    b_half()
     p_step(3)
     work(2)
-    b_half()
     p_step(4)
     work(2)
     c_back()
@@ -480,8 +472,6 @@
     basis_o[...] += dot(upper[pl.ds(pl.multiple_of(z * 48, 16), 48), :], tmat[...])
     p_finish()
     a_finish()
-    for copy in (a_pair, a_spread, a_half):
-        copy.wait_send()
     b_finish()
     c_finish()
 
@@ -504,11 +494,11 @@
             pltpu.VMEM((1024, 2048), BF),
             pltpu.VMEM((3, 64, 256), BF),
             pltpu.VMEM((3, 32, 64, 256), BF),
-            f32(3, 16, 64, 256), f32(3, 13, 64, 256), f32(3, 2, 64, 256), f32(3, 2, 64, 256), f32(64, 256),
+            f32(3, 16, 64, 256), f32(3, 8, 64, 256), f32(3, 7, 64, 256), f32(64, 256),
             pltpu.VMEM((16, 32, 1024), BF), f32(16, 64, 256),
-            f32(2, 16, 512), f32(16, 512), f32(16, 512), f32(16, 16, 512), f32(2, 16, 16, 512),
+            f32(2, 16, 16, 512), f32(16, 16, 512), f32(16, 16, 512), f32(16, 16, 512), f32(16, 512), f32(2, 16, 16, 512),
             f32(512, 512), f32(128, 128), f32(128, 128), f32(768, 512),
-            pltpu.VMEM((3, 1024, 256), BF),
+            pltpu.VMEM((3, 1024, 256), BF), f32(512, 256),
             f32(2, 16, 16, 256), f32(16, 16, 256), f32(16, 16, 256), f32(16, 16, 256), f32(16, 16, 256),
             f32(16, 256), f32(16, 256), f32(2, 16, 16, 256),
             f32(2, 16, 8, 256), f32(16, 8, 256), f32(16, 8, 256), f32(16, 8, 256), f32(16, 8, 256),
@@ -516,12 +506,10 @@
             f32(256, 512), f32(256, 512), f32(256, 256), f32(256, 256), f32(256, 256), f32(768, 256),
             f32(256, 1024), dma((4,)),
             dma((3,)), dma((3,)), dma((3,)), dma((3,)),
-            dma((3, 3)), dma((3, 5)),
+            dma((3, 2, 8, 2)), dma((3, 2, 8, 2)),
             dma((2, 8)), dma((2, 8)),
             dma((2, 8)), dma((2, 8)),
-            dma((2, 8)), dma((2, 8)),
-            dma((3,)), dma((3,)),
-            dma((5,)), dma((5,)), dma((5,)), dma((5,)),
+            dma((5,)), dma((5,)), dma((5,)), dma((5,)), dma((5,)), dma((5,)),
         ],
         compiler_params=pltpu.CompilerParams(
             collective_id=0, has_side_effects=True, vmem_limit_bytes=56 << 20

time: 221 us -> 195 us (0.88)
  Pallas kernels: 214 us -> 188 us
    pallas_call x1, Pallas kernels: 214 us -> 188 us  [body(): pl.pallas_call(comm_kernel, out_shape=(out((64, 256), F32), out((48, 1024...]
where the time goes in v4:
time: 195 us; the launch traced here: 191 us
  Pallas kernels  188 us (96%)
  local copies, waits for them, and re-layouts  3.09 us (2%)
    pallas_call x1, Pallas kernels, body(): pl.pallas_call(comm_kernel, out_shape=(out((64, 256), F32), out((48, 1024...  188 us

profile of v4, /device:TPU:1, one launch (start us, length us, event | category | flops | bytes accessed | tf_op | source)
XLA Modules:
  0.0 191.4 jit_solution(2210388171237975437)
XLA Ops:
  0.6 187.7 %sign_step.1 = (f32[64,256]{1,0:T(8,128)}, f32[48,1024]{1,0:T(8,128)}) custom-call(bf16[32,1,64,1024]{3,2,1,0:T(8,128)(2,1)} %x.1, bf16[64,256]{1,0:T(8,128)(2,1)} %v.1, bf16[32,1024]{1,0:T(8,128)(2,1)} %old.1), custom_call_target="tpu_custom_call" | custom-call | tf_op jit(solution)/shard_map/sign_step/pallas_call | solution.py:487
  188.3 1.5 copy.7
  189.8 1.6 copy.8

commit v5 on v4

--- a/solution.py
+++ b/solution.py
@@ -401,9 +401,7 @@
             b_start()
         if s == 3:
             b_plane()
-        if s == 6:
-            b_column()
-        if s in (4, 5, 7):
+        if s in (4, 5, 6):
             work(1)
 
     third = reduce_scatter(2, hook2)
@@ -419,6 +417,7 @@
     p_step(0)
     pall[z] = panel
     c_plane()
+    b_column()
 
     def to_lower():
         b_ready()
@@ -443,18 +442,18 @@
         tmat[...] = res
 
     items.extend([to_lower, to_square, to_onto, to_old_rows])
-    b_back()
     p_step(1)
     work(3)
     c_column()
     p_step(2)
     work(2)
-    b_half()
+    b_back()
     p_step(3)
     work(2)
     p_step(4)
     work(2)
     c_back()
+    b_half()
     p_step(5)
     work(2)
     p_step(6)
@@ -462,11 +461,13 @@
     c_half()
     p_step(7)
     work(100)
+    c_ready()
+    gram2[...] = cout[...].reshape(256, 256) - square[...]
+    last = factor_items(gram2, inv2, turning, done, 2, 1)
+    last[0]()
     p_step(8)
     to_rest()
-    c_ready()
-    gram2[...] = cout[...].reshape(256, 256) - square[...]
-    for item in factor_items(gram2, inv2, turning, done, 2, 1):
+    for item in last[1:]:
         item()
     upper[512:768, :] = inv2[...]
     basis_o[...] += dot(upper[pl.ds(pl.multiple_of(z * 48, 16), 48), :], tmat[...])

time: 195 us -> 193 us (0.990); the launches traced: 191 us -> 193 us
  no operation moved by 1% of the time
where the time goes in v5:
time: 193 us
  Pallas kernels  189 us (98%)
  local copies, waits for them, and re-layouts  3.09 us (2%)
    pallas_call x1, Pallas kernels, body(): pl.pallas_call(comm_kernel, out_shape=(out((64, 256), F32), out((48, 1024...  189 us

profile of v5, /device:TPU:1, one launch (start us, length us, event | category | flops | bytes accessed | tf_op | source)
XLA Modules:
  0.0 193.1 jit_solution(14035802942152503682)
XLA Ops:
  0.6 189.4 %sign_step.1 = (f32[64,256]{1,0:T(8,128)}, f32[48,1024]{1,0:T(8,128)}) custom-call(bf16[32,1,64,1024]{3,2,1,0:T(8,128)(2,1)} %x.1, bf16[64,256]{1,0:T(8,128)(2,1)} %v.1, bf16[32,1024]{1,0:T(8,128)(2,1)} %old.1), custom_call_target="tpu_custom_call" | custom-call | tf_op jit(solution)/shard_map/sign_step/pallas_call | solution.py:488
  190.0 1.5 copy.7
  191.5 1.6 copy.8
